TPU v7x, 512 devices: a whole 4x8x8 slice. The times are simulated.
512 devices in a mesh: pairs: 64 (over x, z, core), virt: 8 (over y).
Axes of the slice: x: 4, y: 8, z: 8, core: 2. Of those that a mesh axis runs over, the one named last changes fastest.
Arguments:
- amplitudes: bfloat16 [1024, 384, 384], P(('pairs', 'virt')), may hold values from -6 to 6
- factors: bfloat16 [2, 32, 128, 4096], P(None, None, 'virt', 'pairs'), may hold values from -0.21875 to 0.21875
- tiles: int32 [1024, 3], P('pairs'), may hold values from 0 to 31, as said below
- mirror: int32 [1024], P(('pairs', 'virt')), may hold values from 0 to 1023, as said below
- pair_energy: float32 [1024], P(('pairs', 'virt')), may hold values from -3 to -0.5
- virt_energy: float32 [4096], replicated, may hold values from 0.5 to 3
Outputs:
- residual: float32 [1024, 384, 384], P(('pairs', 'virt'))
- updated: bfloat16 [1024, 384, 384], P(('pairs', 'virt'))
Inputs may be any that keep to these rules, and one draw needn't show every extreme that they name: Each row names 3 different tiles; a pair and its mirror name the same tiles in the same order. mirror is an involution without fixed points; the mirror of a pair on a device lies on the device with the same index of virt and the index of pairs half the pairs axis away.
All inputs are finite; a program needn't handle non-finite values.
Results may differ from a plain program's by a relative error of at most 0.005.
Values may be sent and summed in bfloat16 or wider, within the bound.
No kernel may reach another device: no remote copies, remote signals or barrier semaphores. Data moves between devices by JAX's collectives and lax.ppermute only.
A program may use at most 128 MiB of HBM per device.

v0:
```python
import jax
import jax.numpy as jnp
from jax import lax
from jax.sharding import PartitionSpec as P

V = 128
K = 3


def passed_along(block, axis, distance):
    devices = range(lax.axis_size(axis))
    route = [((i - distance) % len(devices), i) for i in devices]
    return lax.ppermute(block, axis, route)


def ladder_of(domain, pair_amps):
    half_ladder = jnp.einsum(
        "qpxy,pyz->qpxz", domain, pair_amps, preferred_element_type=jnp.float32
    ).astype(jnp.bfloat16)
    return jnp.einsum("qpxz,qpwz->pxw", half_ladder, domain, preferred_element_type=jnp.float32)


def shards(amplitudes, factors, tiles, mirror, pair_energy, virt_energy):
    pair_count = amplitudes.shape[0]
    pair_width = amplitudes.shape[1]
    fit_count = factors.shape[0]
    tile_count = factors.shape[1]
    band_rows = factors.shape[2]
    group_size = tiles.shape[0]
    column_strip = lax.all_gather(factors, "pairs", axis=3, tiled=True)
    factor_grid = column_strip.reshape(fit_count, tile_count, band_rows, tile_count, V)
    picked = factor_grid[:, tiles[:, :, None], :, tiles[:, None, :], :]
    band_blocks = picked.transpose(3, 0, 1, 4, 2, 5).reshape(
        fit_count, group_size, K, band_rows, pair_width
    )
    arranged = band_blocks.reshape(
        fit_count, lax.axis_size("virt"), pair_count, K, band_rows, pair_width
    )
    received = lax.all_to_all(arranged, "virt", split_axis=1, concat_axis=4, tiled=True)
    domain = received.reshape(fit_count, pair_count, pair_width, pair_width)
    ladder = ladder_of(domain, amplitudes)
    shift_by = lax.axis_size("pairs") // 2
    mirror_slot = mirror % pair_count
    partner = passed_along(ladder.astype(jnp.bfloat16), "pairs", shift_by).astype(ladder.dtype)
    partner_ladder = jnp.take(partner, mirror_slot, axis=0)
    residual = ladder + jnp.swapaxes(partner_ladder, 1, 2)
    own_tiles = lax.dynamic_slice_in_dim(tiles, lax.axis_index("virt") * pair_count, pair_count, 0)
    energies = jnp.take(virt_energy.reshape(tile_count, V), own_tiles, axis=0).reshape(
        pair_count, pair_width
    )
    denominators = energies[:, :, None] + energies[:, None, :] - pair_energy[:, None, None]
    updated = (amplitudes.astype(jnp.float32) - residual / denominators).astype(jnp.bfloat16)
    return (residual, updated)


def solution(mesh):
    return jax.shard_map(
        shards,
        mesh=mesh,
        in_specs=(
            P(("pairs", "virt"), None, None),
            P(None, None, "virt", "pairs"),
            P("pairs", None),
            P(("pairs", "virt")),
            P(("pairs", "virt")),
            P(),
        ),
        out_specs=(P(("pairs", "virt"), None, None), P(("pairs", "virt"), None, None)),
        check_vma=False,
    )
```

profile of v0, /device:TPU:1, one launch (start us, length us, event | category | flops | bytes accessed | tf_op | source)
XLA Modules:
  0.0 285.0 jit_solution(4439223786803167159)
XLA Ops:
  7.2 0.0 all-gather.2.cloned.1.call-start
  7.2 2.6 copy.27
  9.8 0.0 all-gather.2.cloned.1.call-update
  9.9 0.1 copy.30
  10.0 0.1 copy.29
  10.1 0.1 broadcast_or_fusion
  10.2 0.1 reshape.65
  10.3 156.3 %all-gather.2.cloned.1.call-done = bf16[2,32,16,4096]{1,2,0,3:T(8,128)(2,1)} async-done(((bf16[2,32,16,64]{1,2,0,3:T(8,128)(2,1)}), bf16[2,32,16,4096]{1,2,0,3:T(8,128)(2,1)}) %all-gather.2.cloned.1.call-update) | async-done | bytes 8388624 | tf_op jit(solution)/shard_map/all_gather | solution.py:30
  166.6 40.0 %copy.31 = bf16[2,32,16,32,128]{4,2,3,1,0:T(8,128)(2,1)} copy(bf16[2,32,16,32,128]{1,2,0,4,3:T(8,128)(2,1)} %bitcast.41) | data formatting | bytes 16777216 | tf_op jit(solution)/shard_map/reshape | solution.py:31
  206.7 5.2 %gather_fusion = bf16[144,2,16,128]{3,2,1,0:T(8,128)(2,1)S(1)} fusion(bf16[2,32,16,32,128]{4,2,3,1,0:T(8,128)(2,1)} %copy.31, s32[144]{0:T(256)S(1)} %reshape.65), kind=kCustom, calls=%fused_computation | custom fusion | bytes 2360448 | tf_op jit(solution)/shard_map/gather | solution.py:32
  211.8 1.1 copy.32
  212.9 1.1 reshape_reshape.3
  214.0 1.2 copy.33
  215.2 6.5 %all-to-all-start = ((bf16[2,8,2,3,16,384]{5,4,3,2,0,1:T(8,128)(2,1)}), bf16[2,8,2,3,16,384]{5,4,3,2,0,1:T(8,128)(2,1)S(1)}, u32[]{:S(2)}, u32[]{:S(2)}) async-start(bf16[2,8,2,3,16,384]{5,4,3,2,0,1:T(8,128)(2,1)} %copy.33), calls=%async_computation | async-start | bytes 2359296 | tf_op jit(solution)/shard_map/all_to_all | solution.py:39
  221.6 0.6 compare_and_fusion
  222.2 0.1 copy.37
  222.3 0.7 reshape.81
  223.0 30.7 %all-to-all-done = bf16[2,8,2,3,16,384]{5,4,3,2,0,1:T(8,128)(2,1)S(1)} async-done(((bf16[2,8,2,3,16,384]{5,4,3,2,0,1:T(8,128)(2,1)}), bf16[2,8,2,3,16,384]{5,4,3,2,0,1:T(8,128)(2,1)S(1)}, u32[]{:S(2)}, u32[]{:S(2)}) %all-to-all-start) | async-done | bytes 1179680 | tf_op jit(solution)/shard_map/all_to_all | solution.py:39
  253.7 0.2 copy.34
  253.9 2.6 fusion.9
  256.4 3.1 %collective-permute-start = (bf16[2,384,384]{2,1,0:T(8,128)(2,1)S(1)}, bf16[2,384,384]{2,1,0:T(8,128)(2,1)S(1)}, u32[]{:S(2)}, u32[]{:S(2)}) collective-permute-start(bf16[2,384,384]{2,1,0:T(8,128)(2,1)S(1)} %get-tuple-element.10), channel_id=1, source_target_pairs={{256,0},{264,8},{272,16},{280,24},{288,32},{296,40},{304,48},{312,... | collective-permute-start | bytes 1769480 | tf_op jit(solution)/shard_map/ppermute | solution.py:13
  259.5 0.6 gather_fusion.2
  260.1 0.1 copy.36
  260.2 0.1 select_bitcast_fusion
  260.3 0.6 copy.44
  260.9 0.5 compare_and_fusion.1
  261.4 0.6 pad_clamp_fusion.1
  262.0 12.2 %collective-permute-done = bf16[2,384,384]{2,1,0:T(8,128)(2,1)S(1)} collective-permute-done((bf16[2,384,384]{2,1,0:T(8,128)(2,1)S(1)}, bf16[2,384,384]{2,1,0:T(8,128)(2,1)S(1)}, u32[]{:S(2)}, u32[]{:S(2)}) %collective-permute-start) | collective-permute-done | bytes 589856 | tf_op jit(solution)/shard_map/ppermute | solution.py:13
  274.2 0.1 convert_element_type.21
  274.3 0.7 gather_fusion.1
  275.1 0.4 copy.35
  275.5 2.7 subtract_convert_fusion
  (13 shorter events, 0.1 us)
Async XLA Ops:
  7.2 252.4 %copy-start = (f32[4096]{0:T(1024)S(1)}, f32[4096]{0:T(1024)}, u32[]{:S(2)}) copy-start(f32[4096]{0:T(1024)} %param.11) | copy-start | bytes 49156
  7.2 2.7 copy-start.1
  7.2 159.4 %all-gather.2.cloned.1.call-start = ((), (), s32[]{:S(2)}) async-start(), calls=%async_computation.1 | async-start | bytes 34078720 | tf_op jit(solution)/shard_map/all_gather | solution.py:30
  215.2 38.5 %all-to-all-start = ((bf16[2,8,2,3,16,384]{5,4,3,2,0,1:T(8,128)(2,1)}), bf16[2,8,2,3,16,384]{5,4,3,2,0,1:T(8,128)(2,1)S(1)}, u32[]{:S(2)}, u32[]{:S(2)}) async-start(bf16[2,8,2,3,16,384]{5,4,3,2,0,1:T(8,128)(2,1)} %copy.33), calls=%async_computation | async-start | bytes 2359296 | tf_op jit(solution)/shard_map/all_to_all | solution.py:39
  253.8 5.7 %copy-start.3 = (s32[6]{0:T(128)S(1)}, s32[6]{0:T(128)}, u32[]{:S(2)}) copy-start(s32[6]{0:T(128)} %reshape.81) | copy-start | bytes 76
  253.8 6.3 %copy-start.2 = (pred[2,3]{0,1:T(4,128)(4,1)S(1)}, pred[2,3]{0,1:T(4,128)(4,1)}, u32[]{:S(2)}) copy-start(pred[2,3]{0,1:T(4,128)(4,1)} %get-tuple-element.4) | copy-start | bytes 22
  253.9 7.0 %copy-start.4 = (s32[2]{0:T(128)S(1)}, s32[2]{0:T(128)}, u32[]{:S(2)}) copy-start(s32[2]{0:T(128)} %param.9) | copy-start | bytes 28
  256.4 17.8 %collective-permute-start = (bf16[2,384,384]{2,1,0:T(8,128)(2,1)S(1)}, bf16[2,384,384]{2,1,0:T(8,128)(2,1)S(1)}, u32[]{:S(2)}, u32[]{:S(2)}) collective-permute-start(bf16[2,384,384]{2,1,0:T(8,128)(2,1)S(1)} %get-tuple-element.10), channel_id=1, source_target_pairs={{256,0},{264,8},{272,16},{280,24},{288,32},{296,40},{304,48},{312,... | collective-permute-start | bytes 1769480 | tf_op jit(solution)/shard_map/ppermute | solution.py:13
Sparse Core Ops, SparseCore 0:
  12.0 154.6 all-gather.1
where the time goes:
time: 286 us; the launch traced here: 285 us
  waiting for transfers between devices  199 us (70%)
  local copies, waits for them, and re-layouts  54.7 us (19%)
  between operations  14.2 us (5%)
  starting transfers between devices  9.57 us (3%)
  other arithmetic  4.67 us (2%)
    all_gather x1, waiting for transfers between devices, shards(): column_strip = lax.all_gather(factors, 'pairs', axis=3, tiled=True)  156 us
    reshape x1, local copies, waits for them, and re-layouts, shards(): column_strip.reshape(fit_count, tile_count, band_rows, tile_count, V)  40 us
    all_to_all x1, waiting for transfers between devices, shards(): lax.all_to_all(arranged, 'virt', split_axis=1, concat_axis=4, tiled=True)  30.7 us
    ppermute x1, waiting for transfers between devices, passed_along(): return lax.ppermute(block, axis, route)  12.2 us
    all_to_all x1, starting transfers between devices, shards(): lax.all_to_all(arranged, 'virt', split_axis=1, concat_axis=4, tiled=True)  6.46 us
  transfers between devices with their start and end apart: 3, of which 3 were waited for; matrix products, arithmetic and copies ran while one was open for 1% of the time, Pallas kernels for 0%

commit v1 on v0

v1 whole, which is shorter than its diff:
```python
import functools

import jax
import jax.numpy as jnp
from jax import lax
from jax.experimental import pallas as pl
from jax.experimental.pallas import tpu as pltpu
from jax.sharding import Mesh, PartitionSpec as P

V = 128
K = 3
NX, NZ, NC, NY = 4, 8, 2, 8
NT = 32
NQ = 2
HALF = V // 2
GROUP = 16
WIDTH = K * V
SOURCES = NX * NZ * NC
PLANE = NZ * NC * NY
MSG1 = NT + 2
MSG2 = 2 * K * K
SMEM = pltpu.MemorySpace.SMEM
VMEM = pltpu.MemorySpace.VMEM
PARAMS = pltpu.CompilerParams(vmem_limit_bytes=24 * 1024 * 1024)


def spread_kernel(tiles_ref, factors_ref, out_ref, wide, staged):
    wide[...] = factors_ref[...].astype(jnp.float32).reshape(NQ * NT * 16, HALF)
    lane = lax.broadcasted_iota(jnp.int32, (2, V), 1)
    tile_row = jnp.zeros((2, V), jnp.float32)
    for member in range(GROUP):
        for k in range(K):
            tile_row = jnp.where(
                lane == member * K + k, tiles_ref[k, member].astype(jnp.float32), tile_row
            )
    for z in range(NZ):
        for q in range(NQ):
            base = (z * NQ + q) * MSG1
            for part in range(NT // 8):
                first = (q * NT + part * 8) * 16 + z
                upper = wide[pl.ds(first, 8, stride=16), :]
                lower = wide[pl.ds(first + 8, 8, stride=16), :]
                staged[pl.ds(base + part * 8, 8), :] = jnp.concatenate([upper, lower], axis=1)
            staged[pl.ds(base + NT, 2), :] = tile_row
    packed = staged[...].astype(jnp.bfloat16)
    for x in range(NX):
        out_ref[x] = packed


def select_kernel(info_ref, held_ref, out_ref, wide, staged, tile_rows, tiles, sem):
    wide[...] = held_ref[...].astype(jnp.float32)
    first = info_ref[0] * (GROUP * MSG1) + NT
    for group in range(GROUP):
        tile_rows[pl.ds(group, 1), :] = wide[pl.ds(first + group * MSG1, 1), :].astype(jnp.int32)
    copy = pltpu.make_async_copy(tile_rows, tiles, sem)
    copy.start()
    copy.wait()
    offset = info_ref[1] * K

    def one_group(group, carry):
        for y in range(NY):
            named = [tiles[group, offset + 2 * K * y + k] for k in range(K)]
            base = group * (NY * MSG2) + y * MSG2
            for l in range(K):
                strip = named[l] * (2 * MSG1)
                for k in range(K):
                    row = strip + named[k]
                    for h in range(2):
                        staged[pl.ds(base + (l * 2 + h) * K + k, 1), :] = wide[
                            pl.ds(row + h * MSG1, 1), :
                        ]
        return carry

    lax.fori_loop(0, GROUP, one_group, 0)
    out_ref[...] = staged[...].astype(jnp.bfloat16)


def ladder_kernel(info_ref, amps_ref, mirror_amps_ref, blocks_ref, ladder_ref, sent_ref, wide, domain):
    wide[...] = blocks_ref[...].astype(jnp.float32)
    left = lax.broadcasted_iota(jnp.int32, (NZ, V), 1) < HALF
    for q in range(NQ):
        for y in range(NY):
            for l in range(K):
                for k in range(K):
                    first = (q * NY + y) * MSG2 + l * 2 * K + k
                    stride = NC * NY * MSG2
                    here = wide[pl.ds(first, NZ, stride=stride), :]
                    there = wide[pl.ds(first + K, NZ, stride=stride), :]
                    upper = jnp.where(left, here, pltpu.roll(there, HALF, 1))
                    lower = jnp.where(left, pltpu.roll(here, HALF, 1), there)
                    domain[q, pl.ds(k * V + y * 16, 16), pl.ds(l * V, V)] = jnp.concatenate(
                        [upper, lower], axis=0
                    ).astype(jnp.bfloat16)
    own = amps_ref[info_ref[2]]
    mirrored = mirror_amps_ref[...]
    total = jnp.zeros((WIDTH, WIDTH), jnp.float32)
    across = (((1,), (1,)), ((), ()))
    for q in range(NQ):
        part = domain[q]
        half = jnp.dot(part, own, preferred_element_type=jnp.float32)
        half = half + lax.dot_general(part, mirrored, across, preferred_element_type=jnp.float32)
        total = total + lax.dot_general(
            half.astype(jnp.bfloat16), part, across, preferred_element_type=jnp.float32
        )
    ladder_ref[...] = total
    sent_ref[...] = total.astype(jnp.bfloat16)


def update_block(info_ref, tiles_ref, pair_energy_ref, energy_ref, slot, residual, amps_ref, residual_ref, updated_ref):
    member = 2 * info_ref[3] + slot
    step = pl.program_id(0)
    across = jnp.concatenate([energy_ref[pl.ds(tiles_ref[k, member], 1), :] for k in range(K)], axis=1)
    down = energy_ref[pl.ds(tiles_ref[step, member], 1), :]
    down = jnp.transpose(jnp.broadcast_to(down, (V, V)))
    down = jnp.concatenate([down] * K, axis=1)
    denominators = down + across - pair_energy_ref[slot]
    residual_ref[0] = residual
    updated_ref[0] = (amps_ref[0].astype(jnp.float32) - residual / denominators).astype(jnp.bfloat16)


def own_kernel(info_ref, tiles_ref, pair_energy_ref, energy_ref, ladder_ref, amps_ref, residual_ref, updated_ref):
    update_block(
        info_ref, tiles_ref, pair_energy_ref, energy_ref, info_ref[2], ladder_ref[...],
        amps_ref, residual_ref, updated_ref,
    )


def other_kernel(
    info_ref, tiles_ref, pair_energy_ref, energy_ref, ladder_ref, amps_ref, res_in, upd_in, residual_ref, updated_ref
):
    update_block(
        info_ref, tiles_ref, pair_energy_ref, energy_ref, 1 - info_ref[2],
        jnp.transpose(ladder_ref[...].astype(jnp.float32)), amps_ref, residual_ref, updated_ref,
    )


def whole(space=VMEM):
    return pl.BlockSpec(memory_space=space)


def shards(amplitudes, factors, tiles, mirror, pair_energy, virt_energy):
    f32, bf16 = jnp.float32, jnp.bfloat16
    x = lax.axis_index("x")
    sel = jnp.where(x < NX // 2, 0, 1 - mirror[0] % 2)
    info = jnp.stack([x % (NX // 2), x // (NX // 2), sel, lax.axis_index("y")]).astype(jnp.int32)
    tiles_t = tiles.T

    spread = pl.pallas_call(
        spread_kernel,
        out_shape=jax.ShapeDtypeStruct((NX, NZ * NC * MSG1, V), bf16),
        in_specs=[whole(SMEM), whole()],
        out_specs=whole(),
        scratch_shapes=[pltpu.VMEM((NQ * NT * 16, HALF), f32), pltpu.VMEM((NZ * NC * MSG1, V), f32)],
        compiler_params=PARAMS,
        name="spread",
    )(tiles_t, factors)
    held = lax.all_to_all(
        spread.reshape(SOURCES, MSG1 // 2, 2, V), ("x", "z", "c"), 0, 0, tiled=True
    )
    going = lax.dynamic_index_in_dim(amplitudes, 1 - sel, 0, keepdims=False)
    opposite = [((i + NX // 2) % NX, i) for i in range(NX)]
    mirror_amps = lax.ppermute(going, "x", opposite)

    selected = pl.pallas_call(
        select_kernel,
        out_shape=jax.ShapeDtypeStruct((PLANE * MSG2, V), bf16),
        in_specs=[whole(SMEM), whole()],
        out_specs=whole(),
        scratch_shapes=[
            pltpu.VMEM((SOURCES * MSG1, V), f32),
            pltpu.VMEM((PLANE * MSG2, V), f32),
            pltpu.VMEM((GROUP, V), jnp.int32),
            pltpu.SMEM((GROUP, V), jnp.int32),
            pltpu.SemaphoreType.DMA,
        ],
        compiler_params=PARAMS,
        name="select",
    )(info, held.reshape(SOURCES * MSG1, V))
    blocks = lax.all_to_all(
        selected.reshape(PLANE, MSG2 // 2, 2, V), ("z", "c", "y"), 0, 0, tiled=True
    )

    ladder, sent = pl.pallas_call(
        ladder_kernel,
        out_shape=(
            jax.ShapeDtypeStruct((WIDTH, WIDTH), f32),
            jax.ShapeDtypeStruct((WIDTH, WIDTH), bf16),
        ),
        in_specs=[whole(SMEM), whole(), whole(), whole()],
        out_specs=(whole(), whole()),
        scratch_shapes=[pltpu.VMEM((PLANE * MSG2, V), f32), pltpu.VMEM((NQ, WIDTH, WIDTH), bf16)],
        compiler_params=PARAMS,
        name="ladder",
    )(info, amplitudes, mirror_amps, blocks.reshape(PLANE * MSG2, V))
    received = lax.ppermute(sent, "x", opposite)

    energies = virt_energy.reshape(NT, V)
    outs = (
        jax.ShapeDtypeStruct(amplitudes.shape, f32),
        jax.ShapeDtypeStruct(amplitudes.shape, bf16),
    )

    def band(pick):
        return pl.BlockSpec((1, V, WIDTH), lambda i, info_ref: (pick(info_ref[2]), i, 0))

    def common(body, pick, ladder_spec, extra):
        return pl.pallas_call(
            body,
            out_shape=outs,
            grid_spec=pltpu.PrefetchScalarGridSpec(
                num_scalar_prefetch=1,
                grid=(K,),
                in_specs=[whole(SMEM), whole(SMEM), pl.BlockSpec((NT, V), lambda i, info_ref: (0, 0)), ladder_spec, band(pick)]
                + extra,
                out_specs=(band(pick), band(pick)),
            ),
            input_output_aliases={6: 0, 7: 1} if extra else {},
            cost_estimate=pl.CostEstimate(flops=3 * WIDTH * WIDTH, bytes_accessed=10 * WIDTH * WIDTH, transcendentals=0),
            compiler_params=PARAMS,
            name="own" if not extra else "other",
        )

    residual, updated = common(
        own_kernel, lambda s: s, pl.BlockSpec((V, WIDTH), lambda i, info_ref: (i, 0)), []
    )(info, tiles_t, pair_energy, energies, ladder, amplitudes)
    residual, updated = common(
        other_kernel,
        lambda s: 1 - s,
        pl.BlockSpec((WIDTH, V), lambda i, info_ref: (0, i)),
        [whole(pl.ANY), whole(pl.ANY)],
    )(info, tiles_t, pair_energy, energies, received, amplitudes, residual, updated)
    return (residual, updated)


def solution(mesh):
    fine = Mesh(mesh.devices.reshape(NX, NZ, NC, NY), ("x", "z", "c", "y"))
    pairs = ("x", "z", "c")
    return jax.shard_map(
        shards,
        mesh=fine,
        in_specs=(
            P(pairs + ("y",), None, None),
            P(None, None, "y", pairs),
            P(pairs, None),
            P(pairs + ("y",)),
            P(pairs + ("y",)),
            P(),
        ),
        out_specs=(P(pairs + ("y",), None, None), P(pairs + ("y",), None, None)),
        check_vma=False,
    )
```

time: 286 us -> 90 us (0.31)
  waiting for transfers between devices: 199 us -> 40.8 us
  local copies, waits for them, and re-layouts: 54.7 us -> 1.7 us
  starting transfers between devices: 9.57 us -> 32.5 us
  Pallas kernels: 0 us -> 13.6 us
  between operations: 14.2 us -> 0.92 us
  other arithmetic: 4.67 us -> 0.08 us
    all_gather x1 -> x0, waiting for transfers between devices: 156 us -> none  [shards(): column_strip = lax.all_gather(factors, 'pairs', axis=3, tiled=True)]
    reshape x1 -> x0, local copies, waits for them, and re-layouts: 40 us -> none  [shards(): column_strip.reshape(fit_count, tile_count, band_rows, tile_count, V)]
    all_to_all x1 -> x2, starting transfers between devices: 6.46 us -> 26.1 us  [the longest x1 14.8 us: shards(): lax.all_to_all(spread.reshape(SOURCES, MSG1 // 2, 2, V), ('x', 'z', 'c'),...]
    pallas_call x0 -> x5, Pallas kernels: none -> 13.6 us  [the longest x1 3.91 us: shards(): pl.pallas_call(select_kernel, out_shape=jax.ShapeDtypeStruct((PLANE * MSG...]
    gather x5 -> x0, local copies, waits for them, and re-layouts: 6.85 us -> none  [the longest x1 5.18 us: shards(): picked = factor_grid[:, tiles[:, :, None], :, tiles[:, None, :], :]]
    ppermute x1 -> x2, starting transfers between devices: 3.07 us -> 6.42 us  [the longest x1 3.21 us: shards(): mirror_amps = lax.ppermute(going, 'x', opposite)]
    all_to_all x1 -> x2, waiting for transfers between devices: 30.7 us -> 27.5 us  [the longest x1 17.8 us: shards(): lax.all_to_all(spread.reshape(SOURCES, MSG1 // 2, 2, V), ('x', 'z', 'c'),...]
    ppermute x1 -> x2, waiting for transfers between devices: 12.2 us -> 13.3 us  [the longest x1 7.81 us: shards(): mirror_amps = lax.ppermute(going, 'x', opposite)]
  transfers between devices with their start and end apart: 3 -> 4, of which waited for: 3 -> 4; matrix products, arithmetic and copies ran while one was open for 1% -> 0% of each run, Pallas kernels for 0% -> 3%
where the time goes in v1:
time: 90 us; the launch traced here: 89.6 us
  waiting for transfers between devices  40.8 us (45%)
  starting transfers between devices  32.5 us (36%)
  Pallas kernels  13.6 us (15%)
  local copies, waits for them, and re-layouts  1.7 us (2%)
  between operations  0.92 us (1%)
    all_to_all x1, waiting for transfers between devices, shards(): lax.all_to_all(spread.reshape(SOURCES, MSG1 // 2, 2, V), ('x', 'z', 'c'),...  17.8 us
    all_to_all x1, starting transfers between devices, shards(): lax.all_to_all(spread.reshape(SOURCES, MSG1 // 2, 2, V), ('x', 'z', 'c'),...  14.8 us
    all_to_all x1, starting transfers between devices, shards(): lax.all_to_all(selected.reshape(PLANE, MSG2 // 2, 2, V), ('z', 'c', 'y'),...  11.3 us
    all_to_all x1, waiting for transfers between devices, shards(): lax.all_to_all(selected.reshape(PLANE, MSG2 // 2, 2, V), ('z', 'c', 'y'),...  9.71 us
    ppermute x1, waiting for transfers between devices, shards(): mirror_amps = lax.ppermute(going, 'x', opposite)  7.81 us
    ppermute x1, waiting for transfers between devices, shards(): received = lax.ppermute(sent, 'x', opposite)  5.45 us
    pallas_call x1, Pallas kernels, shards(): pl.pallas_call(select_kernel, out_shape=jax.ShapeDtypeStruct((PLANE * MSG...  3.91 us
    ppermute x1, starting transfers between devices, shards(): mirror_amps = lax.ppermute(going, 'x', opposite)  3.21 us
  transfers between devices with their start and end apart: 4, of which 4 were waited for; matrix products, arithmetic and copies ran while one was open for 0% of the time, Pallas kernels for 3%

profile of v1, /device:TPU:1, one launch (start us, length us, event | category | flops | bytes accessed | tf_op | source)
XLA Modules:
  0.0 89.6 jit_solution(14298337966510817628)
XLA Ops:
  0.6 0.0 copy-start.6
  0.6 0.0 copy-start.1
  0.6 0.9 %copy-done.1 = bf16[2,32,16,64]{3,2,1,0:T(8,128)(2,1)S(1)} copy-done((bf16[2,32,16,64]{3,2,1,0:T(8,128)(2,1)S(1)}, bf16[2,32,16,64]{3,2,1,0:T(8,128)(2,1)}, u32[]{:S(2)}) %copy-start.1) | copy-done | bytes 131096
  1.6 0.0 copy-start.3
  1.6 0.7 copy-done.3
  2.3 1.6 %spread.1 = bf16[4,544,128]{2,1,0:T(8,128)(2,1)} custom-call(s32[3,16]{1,0:T(4,128)S(1)} %bitcast.18, bf16[2,32,16,64]{3,2,1,0:T(8,128)(2,1)S(1)} %copy-done.1), custom_call_target="tpu_custom_call" | custom-call | tf_op jit(solution)/shard_map/spread/pallas_call | solution.py:148
  3.9 14.8 %all-to-all-start = ((bf16[64,17,2,128]{3,2,1,0:T(2,128)(2,1)}), bf16[64,17,2,128]{3,2,1,0:T(2,128)(2,1)S(1)}, u32[]{:S(2)}, u32[]{:S(2)}) async-start(bf16[64,17,2,128]{3,2,1,0:T(2,128)(2,1)} %bitcast.8), calls=%async_computation | async-start | bytes 1114112 | tf_op jit(solution)/shard_map/all_to_all | solution.py:157
  18.8 0.0 copy-done.6
  18.9 0.0 copy-start
  18.9 0.1 pad_add_fusion.info_ref
  19.0 17.8 %all-to-all-done = bf16[64,17,2,128]{3,2,1,0:T(2,128)(2,1)S(1)} async-done(((bf16[64,17,2,128]{3,2,1,0:T(2,128)(2,1)}), bf16[64,17,2,128]{3,2,1,0:T(2,128)(2,1)S(1)}, u32[]{:S(2)}, u32[]{:S(2)}) %all-to-all-start) | async-done | bytes 557088 | tf_op jit(solution)/shard_map/all_to_all | solution.py:157
  36.8 3.9 %select.9 = bf16[2304,128]{1,0:T(8,128)(2,1)} custom-call(s32[4]{0:T(128)S(1)} %pad_add_fusion.info_ref, bf16[2176,128]{1,0:T(8,128)(2,1)S(1)} %bitcast.15), custom_call_target="tpu_custom_call" | custom-call | tf_op jit(solution)/shard_map/select/pallas_call | solution.py:164
  40.7 11.3 %all-to-all-start.1 = ((bf16[128,9,2,128]{3,2,1,0:T(2,128)(2,1)}), bf16[128,9,2,128]{3,2,1,0:T(2,128)(2,1)S(1)}, u32[]{:S(2)}, u32[]{:S(2)}) async-start(bf16[128,9,2,128]{3,2,1,0:T(2,128)(2,1)} %bitcast.10), calls=%async_computation.1 | async-start | bytes 1179648 | tf_op jit(solution)/shard_map/all_to_all | solution.py:179
  52.0 0.0 copy-start.2
  52.0 0.0 copy-start.4
  52.0 0.0 copy-start.5
  52.1 0.0 copy-done
  52.1 3.2 %collective-permute-start = (bf16[384,384]{1,0:T(8,128)(2,1)S(1)}, bf16[384,384]{1,0:T(8,128)(2,1)S(1)}, u32[]{:S(2)}, u32[]{:S(2)}) collective-permute-start(bf16[384,384]{1,0:T(8,128)(2,1)S(1)} %dynamic-slice_bitcast_fusion), channel_id=1, source_target_pairs={{256,0},{384,128},{0,256},{128,384},{257,1},{385,129},{1,257},{129... | collective-permute-start | bytes 884744 | tf_op jit(solution)/shard_map/ppermute | solution.py:162
  55.3 7.8 %collective-permute-done.mirror_amps_ref = bf16[384,384]{1,0:T(8,128)(2,1)S(1)} collective-permute-done((bf16[384,384]{1,0:T(8,128)(2,1)S(1)}, bf16[384,384]{1,0:T(8,128)(2,1)S(1)}, u32[]{:S(2)}, u32[]{:S(2)}) %collective-permute-start) | collective-permute-done | bytes 294944 | tf_op jit(solution)/shard_map/ppermute | solution.py:162
  63.2 9.7 %all-to-all-done.1 = bf16[128,9,2,128]{3,2,1,0:T(2,128)(2,1)S(1)} async-done(((bf16[128,9,2,128]{3,2,1,0:T(2,128)(2,1)}), bf16[128,9,2,128]{3,2,1,0:T(2,128)(2,1)S(1)}, u32[]{:S(2)}, u32[]{:S(2)}) %all-to-all-start.1) | async-done | bytes 589856 | tf_op jit(solution)/shard_map/all_to_all | solution.py:179
  72.9 2.5 %ladder.1 = (f32[384,384]{1,0:T(8,128)S(1)}, bf16[384,384]{1,0:T(8,128)(2,1)S(1)}) custom-call(s32[4]{0:T(128)S(1)} %pad_add_fusion.info_ref, bf16[2,384,384]{2,1,0:T(8,128)(2,1)S(1)} %copy-done, bf16[384,384]{1,0:T(8,128)(2,1)S(1)} %collective-permute-done.mirror_amps_ref, bf16[2304,128]{1,0:T(8,128)(2,1)S(1)} %bitcast.14), custom_call_target="tpu_custom_call" | custom-call | tf_op jit(solution)/shard_map/ladder/pallas_call | solution.py:183
  75.3 3.2 %collective-permute-start.1 = (bf16[384,384]{1,0:T(8,128)(2,1)S(1)}, bf16[384,384]{1,0:T(8,128)(2,1)S(1)}, u32[]{:S(2)}, u32[]{:S(2)}) collective-permute-start(bf16[384,384]{1,0:T(8,128)(2,1)S(1)} %get-tuple-element.6), channel_id=1, source_target_pairs={{256,0},{384,128},{0,256},{128,384},{257,1},{385,129},{1,257},{129... | collective-permute-start | bytes 884744 | tf_op jit(solution)/shard_map/ppermute | solution.py:195
  78.5 0.0 copy-done.2
  78.5 0.0 copy-done.4
  78.6 0.0 copy-done.5
  78.6 2.7 %own.1 = (f32[2,384,384]{2,1,0:T(8,128)}, bf16[2,384,384]{2,1,0:T(8,128)(2,1)}) custom-call(s32[4]{0:T(128)S(1)} %pad_add_fusion.info_ref, s32[3,16]{1,0:T(4,128)S(1)} %bitcast.19, f32[2]{0:T(128)S(1)} %copy-done.5, f32[32,128]{1,0:T(8,128)S(1)} %bitcast.16, f32[384,384]{1,0:T(8,128)S(1)} %get-tuple-element.7.ladder_ref, bf16[2,384,384]{2,1,0:T(8,128)(2,1)S(1)} %copy-done), custom_call_target="tpu_custom_call" | custom-call | flops 442368 | bytes 1474560 | tf_op jit(solution)/shard_map/own/pallas_call | solution.py:223
  81.3 5.5 %collective-permute-done.1.ladder_ref = bf16[384,384]{1,0:T(8,128)(2,1)S(1)} collective-permute-done((bf16[384,384]{1,0:T(8,128)(2,1)S(1)}, bf16[384,384]{1,0:T(8,128)(2,1)S(1)}, u32[]{:S(2)}, u32[]{:S(2)}) %collective-permute-start.1) | collective-permute-done | bytes 294944 | tf_op jit(solution)/shard_map/ppermute | solution.py:195
  86.7 2.9 %other.1 = (f32[2,384,384]{2,1,0:T(8,128)}, bf16[2,384,384]{2,1,0:T(8,128)(2,1)}) custom-call(s32[4]{0:T(128)S(1)} %pad_add_fusion.info_ref, s32[3,16]{1,0:T(4,128)S(1)} %bitcast.20, f32[2]{0:T(128)S(1)} %copy-done.5, f32[32,128]{1,0:T(8,128)S(1)} %bitcast.17, ...), custom_call_target="tpu_custom_call", output_to_operand_aliasing={{0}: (6, {}), {1}: (7, {})} | custom-call | flops 442368 | bytes 1474560 | tf_op jit(solution)/shard_map/other/pallas_call | solution.py:226
  (1 shorter events, 0.0 us)
Async XLA Ops:
  0.6 18.1 %copy-start.6 = (s32[2]{0:T(128)S(1)}, s32[2]{0:T(128)}, u32[]{:S(2)}) copy-start(s32[2]{0:T(128)} %param.9) | copy-start | bytes 28
  0.6 1.0 %copy-start.1 = (bf16[2,32,16,64]{3,2,1,0:T(8,128)(2,1)S(1)}, bf16[2,32,16,64]{3,2,1,0:T(8,128)(2,1)}, u32[]{:S(2)}) copy-start(bf16[2,32,16,64]{3,2,1,0:T(8,128)(2,1)} %factors_ref.1) | copy-start | bytes 393220
  1.6 0.7 copy-start.3
  3.9 32.9 %all-to-all-start = ((bf16[64,17,2,128]{3,2,1,0:T(2,128)(2,1)}), bf16[64,17,2,128]{3,2,1,0:T(2,128)(2,1)S(1)}, u32[]{:S(2)}, u32[]{:S(2)}) async-start(bf16[64,17,2,128]{3,2,1,0:T(2,128)(2,1)} %bitcast.8), calls=%async_computation | async-start | bytes 1114112 | tf_op jit(solution)/shard_map/all_to_all | solution.py:157
  18.9 33.2 %copy-start = (bf16[2,384,384]{2,1,0:T(8,128)(2,1)S(1)}, bf16[2,384,384]{2,1,0:T(8,128)(2,1)}, u32[]{:S(2)}) copy-start(bf16[2,384,384]{2,1,0:T(8,128)(2,1)} %amps_ref.5) | copy-start | bytes 1769476
  40.7 32.1 %all-to-all-start.1 = ((bf16[128,9,2,128]{3,2,1,0:T(2,128)(2,1)}), bf16[128,9,2,128]{3,2,1,0:T(2,128)(2,1)S(1)}, u32[]{:S(2)}, u32[]{:S(2)}) async-start(bf16[128,9,2,128]{3,2,1,0:T(2,128)(2,1)} %bitcast.10), calls=%async_computation.1 | async-start | bytes 1179648 | tf_op jit(solution)/shard_map/all_to_all | solution.py:179
  52.0 26.5 %copy-start.2 = (f32[4096]{0:T(1024)S(1)}, f32[4096]{0:T(1024)}, u32[]{:S(2)}) copy-start(f32[4096]{0:T(1024)} %param.11) | copy-start | bytes 49156
  52.0 26.5 %copy-start.4 = (s32[16,3]{0,1:T(4,128)S(1)}, s32[16,3]{0,1:T(4,128)}, u32[]{:S(2)}) copy-start(s32[16,3]{0,1:T(4,128)} %param.8) | copy-start | bytes 580
  52.0 26.5 %copy-start.5 = (f32[2]{0:T(128)S(1)}, f32[2]{0:T(128)}, u32[]{:S(2)}) copy-start(f32[2]{0:T(128)} %pair_energy_ref.3) | copy-start | bytes 28
  52.1 11.0 %collective-permute-start = (bf16[384,384]{1,0:T(8,128)(2,1)S(1)}, bf16[384,384]{1,0:T(8,128)(2,1)S(1)}, u32[]{:S(2)}, u32[]{:S(2)}) collective-permute-start(bf16[384,384]{1,0:T(8,128)(2,1)S(1)} %dynamic-slice_bitcast_fusion), channel_id=1, source_target_pairs={{256,0},{384,128},{0,256},{128,384},{257,1},{385,129},{1,257},{129... | collective-permute-start | bytes 884744 | tf_op jit(solution)/shard_map/ppermute | solution.py:162
  75.3 11.4 %collective-permute-start.1 = (bf16[384,384]{1,0:T(8,128)(2,1)S(1)}, bf16[384,384]{1,0:T(8,128)(2,1)S(1)}, u32[]{:S(2)}, u32[]{:S(2)}) collective-permute-start(bf16[384,384]{1,0:T(8,128)(2,1)S(1)} %get-tuple-element.6), channel_id=1, source_target_pairs={{256,0},{384,128},{0,256},{128,384},{257,1},{385,129},{1,257},{129... | collective-permute-start | bytes 884744 | tf_op jit(solution)/shard_map/ppermute | solution.py:195

commit v2 on v0

v2 whole, which is shorter than its diff:
```python
import jax
import jax.numpy as jnp
from jax import lax
from jax.experimental import pallas as pl
from jax.experimental.pallas import tpu as pltpu
from jax.sharding import Mesh, PartitionSpec as P

V = 128
K = 3
NX, NU, NB, NC, NY = 4, 2, 4, 2, 8
NT = 32
NQ = 2
HALF = V // 2
GROUP = 16
WIDTH = K * V
ROWS = NX * NB
SOURCES = NU * ROWS
PLANE = ROWS * NY
MSG1 = NT + 2
HELD = SOURCES * MSG1
MSG2 = 2 * K * K
SMEM = pltpu.MemorySpace.SMEM
VMEM = pltpu.MemorySpace.VMEM
PARAMS = pltpu.CompilerParams(vmem_limit_bytes=24 * 1024 * 1024)


def spread_kernel(tiles_hbm, factors_hbm, out_ref, tiles, raw, wide, staged, sems):
    copies = [pltpu.make_async_copy(tiles_hbm, tiles, sems.at[0])]
    part = NT // 2
    for i in range(2):
        strip = pl.ds(i * part, part)
        copies.append(pltpu.make_async_copy(factors_hbm.at[:, strip], raw.at[:, strip], sems.at[1 + i]))
    for copy in copies:
        copy.start()
    copies[0].wait()
    lane = lax.broadcasted_iota(jnp.int32, (2, V), 1)
    tile_row = jnp.zeros((2, V), jnp.float32)
    for member in range(GROUP):
        for k in range(K):
            tile_row = jnp.where(lane == member * K + k, tiles[k, member].astype(jnp.float32), tile_row)
    for row in range(ROWS):
        staged[pl.ds(row * MSG1 + NT, 2), :] = tile_row
    for i in range(2):
        copies[1 + i].wait()
        for q in range(NQ):
            first = (q * NT + i * part) * ROWS
            wide[pl.ds(first, part * ROWS), :] = (
                raw[q, pl.ds(i * part, part)].astype(jnp.float32).reshape(part * ROWS, HALF)
            )
        for row in range(ROWS):
            for eight in range(part // 8):
                first = (i * part + eight * 8) * ROWS + row
                sides = [wide[pl.ds(q * NT * ROWS + first, 8, stride=ROWS), :] for q in range(NQ)]
                staged[pl.ds(row * MSG1 + i * part + eight * 8, 8), :] = jnp.concatenate(sides, axis=1)
    packed = staged[...].astype(jnp.bfloat16)
    for u in range(NU):
        out_ref[u] = packed


def select_kernel(info_ref, mine_ref, theirs_ref, out_ref, wide, staged, tile_rows, tiles, sem):
    slab = ROWS * MSG1
    core = info_ref[1]
    start = pl.multiple_of(info_ref[0] * slab, 16)
    wide[pl.ds(core, HELD, stride=2), :] = mine_ref[...].astype(jnp.float32)
    first = 2 * (start + NT) + core
    for group in range(GROUP // 2):
        named = wide[pl.ds(first + 2 * group * MSG1, 1), :].astype(jnp.int32)
        tile_rows[pl.ds(group, 1), :] = 2 * named
        place = ((named >> 2) & 1) * ROWS + (named >> 3) * NB + (named & (NB - 1))
        tile_rows[pl.ds(GROUP // 2 + group, 1), :] = 2 * MSG1 * place
    copy = pltpu.make_async_copy(tile_rows, tiles, sem)
    copy.start()
    wide[pl.ds(1 - core, HELD, stride=2), :] = theirs_ref[...].astype(jnp.float32)
    copy.wait()

    def one_group(group, carry):
        for parity in range(2):
            for y in range(NY):
                lanes = [(2 * y + parity) * K + k for k in range(K)]
                named = [tiles[group, lane] for lane in lanes]
                strips = [tiles[GROUP // 2 + group, lane] for lane in lanes]
                base = group * MSG2 + (y * ROWS + parity * (GROUP // 2)) * MSG2
                for l in range(K):
                    for k in range(K):
                        staged[pl.ds(base + (l * K + k) * 2, 2), :] = wide[
                            pl.ds(pl.multiple_of(strips[l] + named[k], 2), 2), :
                        ]
        return carry

    lax.fori_loop(0, GROUP // 2, one_group, 0)
    out_ref[...] = staged[...].astype(jnp.bfloat16)


ACROSS = (((1,), (1,)), ((), ()))


def ladder_kernel(info_ref, amps_ref, mirror_amps_ref, blocks_ref, sent_ref, domain, half, mirror_half, wide):
    wide[...] = blocks_ref[...].astype(jnp.float32)
    left = lax.broadcasted_iota(jnp.int32, (ROWS, V), 1) < HALF
    for y in range(NY):
        for l in range(K):
            for k in range(K):
                first = y * ROWS * MSG2 + (l * K + k) * 2
                sides = [wide[pl.ds(first + h, ROWS, stride=MSG2), :] for h in range(2)]
                rows = pl.ds(k * V + y * ROWS, ROWS)
                for q in range(NQ):
                    block = jnp.where(
                        left,
                        sides[0] if q == 0 else pltpu.roll(sides[0], HALF, 1),
                        sides[1] if q == 1 else pltpu.roll(sides[1], HALF, 1),
                    )
                    domain[rows, pl.ds(q * WIDTH + l * V, V)] = block.astype(jnp.bfloat16)
    own = amps_ref[info_ref[2]]
    mirrored = mirror_amps_ref[...]
    for q in range(NQ):
        columns = pl.ds(q * WIDTH, WIDTH)
        part = domain[:, columns]
        half[:, columns] = jnp.dot(part, own, preferred_element_type=jnp.float32).astype(jnp.bfloat16)
        mirror_half[:, columns] = jnp.dot(part, mirrored, preferred_element_type=jnp.float32).astype(
            jnp.bfloat16
        )
    sent_ref[...] = (
        lax.dot_general(domain[...], half[...], ACROSS, preferred_element_type=jnp.float32)
        + lax.dot_general(mirror_half[...], domain[...], ACROSS, preferred_element_type=jnp.float32)
    ).astype(jnp.bfloat16)


def denominators_of(info_ref, tiles_ref, pair_energy_ref, energy_ref, slot):
    member = 2 * info_ref[3] + slot
    rows = [energy_ref[pl.ds(tiles_ref[k, member], 1), :] for k in range(K)]
    across = jnp.concatenate(rows, axis=1)
    bands = []
    for row in rows:
        down = jnp.transpose(jnp.broadcast_to(row, (V, V)))
        bands.append(jnp.concatenate([down] * K, axis=1) + across - pair_energy_ref[slot])
    return bands


def write_pair(slot, denominator_of, residual_of, amps_ref, residual_out, updated_out, residual_buf, updated_buf, sems):
    copies = []
    for step in range(K):
        band = pl.ds(step * V, V)
        residual = residual_of(band)
        residual_buf[band, :] = residual
        updated_buf[band, :] = (
            amps_ref[slot, band, :].astype(jnp.float32) - residual / denominator_of(step)
        ).astype(jnp.bfloat16)
        for buf, out, sem in (
            (residual_buf, residual_out, sems.at[0, step]),
            (updated_buf, updated_out, sems.at[1, step]),
        ):
            copy = pltpu.make_async_copy(buf.at[band, :], out.at[slot, band, :], sem)
            copy.start()
            copies.append(copy)
    for copy in copies:
        copy.wait()


def own_kernel(
    info_ref, tiles_ref, pair_energy_ref, energy_ref, amps_ref, domain, half, mirror_half,
    residual_out, updated_out, other_ref, residual_buf, updated_buf, sems,
):
    energies = (info_ref, tiles_ref, pair_energy_ref, energy_ref)
    slot = info_ref[2]
    for step, band in enumerate(denominators_of(*energies, 1 - slot)):
        other_ref[pl.ds(step * V, V), :] = band
    bands = denominators_of(*energies, slot)

    def residual_of(band):
        return lax.dot_general(
            half[band, :], domain[...], ACROSS, preferred_element_type=jnp.float32
        ) + lax.dot_general(domain[band, :], mirror_half[...], ACROSS, preferred_element_type=jnp.float32)

    write_pair(
        slot, lambda step: bands[step], residual_of, amps_ref,
        residual_out, updated_out, residual_buf, updated_buf, sems,
    )


def other_kernel(
    info_ref, amps_ref, received_ref, denominators_ref, residual_in, updated_in,
    residual_out, updated_out, residual_buf, updated_buf, sems,
):
    write_pair(
        1 - info_ref[2],
        lambda step: denominators_ref[pl.ds(step * V, V), :],
        lambda band: received_ref[band, :].astype(jnp.float32),
        amps_ref, residual_out, updated_out, residual_buf, updated_buf, sems,
    )


def whole(space=VMEM):
    return pl.BlockSpec(memory_space=space)


def shards(amplitudes, factors, tiles, mirror, pair_energy, virt_energy):
    f32, bf16 = jnp.float32, jnp.bfloat16
    x = lax.axis_index("x")
    sel = jnp.where(x < NX // 2, 0, 1 - (mirror[0] & 1))
    info = jnp.stack([lax.axis_index(a) for a in ("u", "c")] + [sel, lax.axis_index("y")]).astype(jnp.int32)
    tiles_t = tiles.T

    spread = pl.pallas_call(
        spread_kernel,
        out_shape=jax.ShapeDtypeStruct((NU, ROWS * MSG1, V), bf16),
        in_specs=[whole(pltpu.MemorySpace.HBM), whole(pltpu.MemorySpace.HBM)],
        out_specs=whole(),
        scratch_shapes=[
            pltpu.SMEM(tiles_t.shape, jnp.int32),
            pltpu.VMEM(factors.shape, bf16),
            pltpu.VMEM((NQ * NT * ROWS, HALF), f32),
            pltpu.VMEM((ROWS * MSG1, V), f32),
            pltpu.SemaphoreType.DMA((3,)),
        ],
        compiler_params=pltpu.CompilerParams(vmem_limit_bytes=60 * 1024 * 1024),
        name="spread",
    )(tiles_t, factors)
    held = lax.all_to_all(spread.reshape(SOURCES, MSG1 // 2, 2, V), ("u", "x", "b"), 0, 0, tiled=True)
    theirs = lax.ppermute(held, "c", [(1, 0), (0, 1)])
    going = lax.dynamic_index_in_dim(amplitudes, 1 - sel, 0, keepdims=False)
    opposite = [((i + NX // 2) % NX, i) for i in range(NX)]
    mirror_amps = lax.ppermute(going, "x", opposite)

    selected = pl.pallas_call(
        select_kernel,
        out_shape=jax.ShapeDtypeStruct((PLANE * MSG2, V), bf16),
        in_specs=[whole(SMEM), whole(), whole()],
        out_specs=whole(),
        scratch_shapes=[
            pltpu.VMEM((NC * HELD, V), f32),
            pltpu.VMEM((PLANE * MSG2, V), f32),
            pltpu.VMEM((GROUP, V), jnp.int32),
            pltpu.SMEM((GROUP, V), jnp.int32),
            pltpu.SemaphoreType.DMA,
        ],
        compiler_params=PARAMS,
        name="select",
    )(info, held.reshape(HELD, V), theirs.reshape(HELD, V))
    blocks = lax.all_to_all(
        selected.reshape(PLANE, MSG2 // 2, 2, V), ("y", "x", "b"), 0, 0, tiled=True
    )

    wide_half = jax.ShapeDtypeStruct((WIDTH, NQ * WIDTH), bf16)
    sent, domain, half, mirror_half = pl.pallas_call(
        ladder_kernel,
        out_shape=(jax.ShapeDtypeStruct((WIDTH, WIDTH), bf16), wide_half, wide_half, wide_half),
        in_specs=[whole(SMEM), whole(), whole(), whole()],
        out_specs=(whole(),) * 4,
        scratch_shapes=[pltpu.VMEM((PLANE * MSG2, V), f32)],
        compiler_params=PARAMS,
        name="ladder",
    )(info, amplitudes, mirror_amps, blocks.reshape(PLANE * MSG2, V))
    received = lax.ppermute(sent, "x", opposite)

    energies = virt_energy.reshape(NT, V)
    outs = (
        jax.ShapeDtypeStruct(amplitudes.shape, f32),
        jax.ShapeDtypeStruct(amplitudes.shape, bf16),
    )
    buffers = [
        pltpu.VMEM((WIDTH, WIDTH), f32),
        pltpu.VMEM((WIDTH, WIDTH), bf16),
        pltpu.SemaphoreType.DMA((2, K)),
    ]
    residual, updated, denominators = pl.pallas_call(
        own_kernel,
        out_shape=outs + (jax.ShapeDtypeStruct((WIDTH, WIDTH), f32),),
        in_specs=[whole(SMEM)] * 3 + [whole()] * 5,
        out_specs=(whole(pl.ANY), whole(pl.ANY), whole()),
        scratch_shapes=buffers,
        cost_estimate=pl.CostEstimate(flops=8 * WIDTH**3, bytes_accessed=10 * WIDTH**2, transcendentals=0),
        compiler_params=PARAMS,
        name="own",
    )(info, tiles_t, pair_energy, energies, amplitudes, domain, half, mirror_half)
    residual, updated = pl.pallas_call(
        other_kernel,
        out_shape=outs,
        in_specs=[whole(SMEM), whole(), whole(), whole(), whole(pl.ANY), whole(pl.ANY)],
        out_specs=(whole(pl.ANY),) * 2,
        scratch_shapes=buffers,
        input_output_aliases={4: 0, 5: 1},
        cost_estimate=pl.CostEstimate(flops=4 * WIDTH**2, bytes_accessed=10 * WIDTH**2, transcendentals=0),
        compiler_params=PARAMS,
        name="other",
    )(info, amplitudes, received, denominators, residual, updated)
    return (residual, updated)


def solution(mesh):
    fine = Mesh(mesh.devices.reshape(NX, NU, NB, NC, NY), ("x", "u", "b", "c", "y"))
    pairs = ("x", "u", "b", "c")
    return jax.shard_map(
        shards,
        mesh=fine,
        in_specs=(
            P(pairs + ("y",), None, None),
            P(None, None, "y", pairs),
            P(pairs, None),
            P(pairs + ("y",)),
            P(pairs + ("y",)),
            P(),
        ),
        out_specs=(P(pairs + ("y",), None, None), P(pairs + ("y",), None, None)),
        check_vma=False,
    )
```

time: 286 us -> 82.2 us (0.29)
  the two profiles are of different devices: /device:TPU:1 before, /device:TPU:8 now
where the time goes in v2:
time: 82.2 us; the launch traced here: 81.8 us
  blocking collectives  27.1 us (33%)
  waiting for transfers between devices  23.3 us (28%)
  starting transfers between devices  18.5 us (23%)
  Pallas kernels  11.3 us (14%)
  between operations  1.43 us (2%)
    all_to_all x1, blocking collectives, shards(): lax.all_to_all(spread.reshape(SOURCES, MSG1 // 2, 2, V), ('u', 'x', 'b'),...  27.1 us
    ppermute x1, waiting for transfers between devices, shards(): mirror_amps = lax.ppermute(going, 'x', opposite)  12 us
    all_to_all x1, starting transfers between devices, shards(): lax.all_to_all(selected.reshape(PLANE, MSG2 // 2, 2, V), ('y', 'x', 'b'),...  9.78 us
    ppermute x1, waiting for transfers between devices, shards(): received = lax.ppermute(sent, 'x', opposite)  5.64 us
    ppermute x1, starting transfers between devices, shards(): mirror_amps = lax.ppermute(going, 'x', opposite)  4.91 us
    all_to_all x1, waiting for transfers between devices, shards(): lax.all_to_all(selected.reshape(PLANE, MSG2 // 2, 2, V), ('y', 'x', 'b'),...  4.91 us
    pallas_call x1, Pallas kernels, shards(): pl.pallas_call(select_kernel, out_shape=jax.ShapeDtypeStruct((PLANE * MSG...  3.21 us
    pallas_call x1, Pallas kernels, shards(): pl.pallas_call(own_kernel, out_shape=outs + (jax.ShapeDtypeStruct((WIDTH,...  2.51 us
  transfers between devices with their start and end apart: 4, of which 4 were waited for; matrix products, arithmetic and copies ran while one was open for 0% of the time, Pallas kernels for 3%

profile of v2, /device:TPU:8, one launch (start us, length us, event | category | flops | bytes accessed | tf_op | source)
XLA Modules:
  0.0 81.8 jit_solution(16726315039573585993)
XLA Ops:
  0.6 1.9 %spread.1 = bf16[2,544,128]{2,1,0:T(8,128)(2,1)} custom-call(s32[3,16]{1,0:T(4,128)} %bitcast.19, bf16[2,32,16,64]{3,2,1,0:T(8,128)(2,1)} %factors_hbm.1), custom_call_target="tpu_custom_call" | custom-call | tf_op jit(solution)/shard_map/spread/pallas_call | solution.py:203
  2.5 27.1 %all_to_all.10 = bf16[32,17,2,128]{3,2,1,0:T(2,128)(2,1)S(1)} all-to-all(bf16[32,17,2,128]{3,2,1,0:T(2,128)(2,1)} %bitcast.21), channel_id=1, replica_groups=mesh['x'=4,'u'=2,'b'=4,'c'=2,'y'=8] {'u','x','b'}, dimensions={0} | all-to-all | bytes 557056 | tf_op jit(solution)/shard_map/all_to_all | solution.py:218
  29.6 1.9 %collective-permute-start.1 = (bf16[32,17,2,128]{3,2,1,0:T(2,128)(2,1)S(1)}, bf16[32,17,2,128]{3,2,1,0:T(2,128)(2,1)S(1)}, u32[]{:S(2)}, u32[]{:S(2)}) collective-permute-start(bf16[32,17,2,128]{3,2,1,0:T(2,128)(2,1)S(1)} %all_to_all.10), channel_id=1, source_target_pairs={{8,0},{0,8},{9,1},{1,9},{10,2},{2,10},{11,3},{3,11},{12,4},{4,12},... | collective-permute-start | bytes 835592 | tf_op jit(solution)/shard_map/ppermute | solution.py:219
  32.2 0.0 copy-start
  32.2 0.1 pad_add_fusion.info_ref
  32.3 0.8 collective-permute-done.1
  33.1 3.2 %select.1 = bf16[2304,128]{1,0:T(8,128)(2,1)} custom-call(s32[4]{0:T(128)S(1)} %pad_add_fusion.info_ref, bf16[1088,128]{1,0:T(8,128)(2,1)S(1)} %bitcast.16, bf16[1088,128]{1,0:T(8,128)(2,1)S(1)} %bitcast.17), custom_call_target="tpu_custom_call" | custom-call | tf_op jit(solution)/shard_map/select/pallas_call | solution.py:224
  36.3 9.8 %all-to-all-start.1 = ((bf16[128,9,2,128]{3,2,1,0:T(2,128)(2,1)}), bf16[128,9,2,128]{3,2,1,0:T(2,128)(2,1)S(1)}, u32[]{:S(2)}, u32[]{:S(2)}) async-start(bf16[128,9,2,128]{3,2,1,0:T(2,128)(2,1)} %bitcast.10), calls=%async_computation.1 | async-start | bytes 1179648 | tf_op jit(solution)/shard_map/all_to_all | solution.py:239
  46.1 0.0 copy-start.1
  46.1 0.0 copy-start.2
  46.1 0.0 copy-start.3
  46.1 0.0 copy-done
  46.2 4.9 %collective-permute-start = (bf16[384,384]{1,0:T(8,128)(2,1)S(1)}, bf16[384,384]{1,0:T(8,128)(2,1)S(1)}, u32[]{:S(2)}, u32[]{:S(2)}) collective-permute-start(bf16[384,384]{1,0:T(8,128)(2,1)S(1)} %dynamic-slice_bitcast_fusion), channel_id=1, source_target_pairs={{256,0},{384,128},{0,256},{128,384},{257,1},{385,129},{1,257},{129... | collective-permute-start | bytes 884744 | tf_op jit(solution)/shard_map/ppermute | solution.py:222
  51.1 12.0 %collective-permute-done.mirror_amps_ref = bf16[384,384]{1,0:T(8,128)(2,1)S(1)} collective-permute-done((bf16[384,384]{1,0:T(8,128)(2,1)S(1)}, bf16[384,384]{1,0:T(8,128)(2,1)S(1)}, u32[]{:S(2)}, u32[]{:S(2)}) %collective-permute-start) | collective-permute-done | bytes 294944 | tf_op jit(solution)/shard_map/ppermute | solution.py:222
  63.1 4.9 %all-to-all-done.1 = bf16[128,9,2,128]{3,2,1,0:T(2,128)(2,1)S(1)} async-done(((bf16[128,9,2,128]{3,2,1,0:T(2,128)(2,1)}), bf16[128,9,2,128]{3,2,1,0:T(2,128)(2,1)S(1)}, u32[]{:S(2)}, u32[]{:S(2)}) %all-to-all-start.1) | async-done | bytes 589856 | tf_op jit(solution)/shard_map/all_to_all | solution.py:239
  68.0 2.2 %ladder.1 = (bf16[384,384]{1,0:T(8,128)(2,1)S(1)}, bf16[384,768]{1,0:T(8,128)(2,1)S(1)}, bf16[384,768]{1,0:T(8,128)(2,1)S(1)}, bf16[384,768]{1,0:T(8,128)(2,1)S(1)}) custom-call(s32[4]{0:T(128)S(1)} %pad_add_fusion.info_ref, bf16[2,384,384]{2,1,0:T(8,128)(2,1)S(1)} %copy-done, bf16[384,384]{1,0:T(8,128)(2,1)S(1)} %collective-permute-done.mirror_amps_ref, ...), custom_call_target="tpu_custom_call" | custom-call | tf_op jit(solution)/shard_map/ladder/pallas_call | solution.py:244
  70.2 1.9 %collective-permute-start.2 = (bf16[384,384]{1,0:T(8,128)(2,1)S(1)}, bf16[384,384]{1,0:T(8,128)(2,1)S(1)}, u32[]{:S(2)}, u32[]{:S(2)}) collective-permute-start(bf16[384,384]{1,0:T(8,128)(2,1)S(1)} %get-tuple-element.9), channel_id=1, source_target_pairs={{256,0},{384,128},{0,256},{128,384},{257,1},{385,129},{1,257},{129... | collective-permute-start | bytes 884744 | tf_op jit(solution)/shard_map/ppermute | solution.py:253
  72.1 0.0 copy-done.1
  72.1 0.0 copy-done.2
  72.1 0.0 copy-done.3
  72.1 2.5 %own.1 = (f32[2,384,384]{2,1,0:T(8,128)}, bf16[2,384,384]{2,1,0:T(8,128)(2,1)}, f32[384,384]{1,0:T(8,128)S(1)}) custom-call(s32[4]{0:T(128)S(1)} %pad_add_fusion.info_ref, s32[3,16]{1,0:T(4,128)S(1)} %bitcast.20, f32[2]{0:T(128)S(1)} %copy-done.3, f32[32,128]{1,0:T(8,128)S(1)} %bitcast.18, bf16[2,384,384]{2,1,0:T(8,128)(2,1)S(1)} %copy-done, ...), custom_call_target="tpu_custom_call" | custom-call | flops 452984832 | bytes 1474560 | tf_op jit(solution)/shard_map/own/pallas_call | solution.py:265
  74.7 5.6 %collective-permute-done.2.received_ref = bf16[384,384]{1,0:T(8,128)(2,1)S(1)} collective-permute-done((bf16[384,384]{1,0:T(8,128)(2,1)S(1)}, bf16[384,384]{1,0:T(8,128)(2,1)S(1)}, u32[]{:S(2)}, u32[]{:S(2)}) %collective-permute-start.2) | collective-permute-done | bytes 294944 | tf_op jit(solution)/shard_map/ppermute | solution.py:253
  80.3 1.5 %other.1 = (f32[2,384,384]{2,1,0:T(8,128)}, bf16[2,384,384]{2,1,0:T(8,128)(2,1)}) custom-call(s32[4]{0:T(128)S(1)} %pad_add_fusion.info_ref, bf16[2,384,384]{2,1,0:T(8,128)(2,1)S(1)} %copy-done, bf16[384,384]{1,0:T(8,128)(2,1)S(1)} %collective-permute-done.2.received_ref, ...), custom_call_target="tpu_custom_call", output_to_operand_aliasing={{0}: (4, {}), {1}: (5, {})} | custom-call | flops 589824 | bytes 1474560 | tf_op jit(solution)/shard_map/other/pallas_call | solution.py:275
  (1 shorter events, 0.0 us)
Async XLA Ops:
  29.6 3.4 %collective-permute-start.1 = (bf16[32,17,2,128]{3,2,1,0:T(2,128)(2,1)S(1)}, bf16[32,17,2,128]{3,2,1,0:T(2,128)(2,1)S(1)}, u32[]{:S(2)}, u32[]{:S(2)}) collective-permute-start(bf16[32,17,2,128]{3,2,1,0:T(2,128)(2,1)S(1)} %all_to_all.10), channel_id=1, source_target_pairs={{8,0},{0,8},{9,1},{1,9},{10,2},{2,10},{11,3},{3,11},{12,4},{4,12},... | collective-permute-start | bytes 835592 | tf_op jit(solution)/shard_map/ppermute | solution.py:219
  32.2 13.9 %copy-start = (bf16[2,384,384]{2,1,0:T(8,128)(2,1)S(1)}, bf16[2,384,384]{2,1,0:T(8,128)(2,1)}, u32[]{:S(2)}) copy-start(bf16[2,384,384]{2,1,0:T(8,128)(2,1)} %amps_ref.5) | copy-start | bytes 1769476
  36.3 31.7 %all-to-all-start.1 = ((bf16[128,9,2,128]{3,2,1,0:T(2,128)(2,1)}), bf16[128,9,2,128]{3,2,1,0:T(2,128)(2,1)S(1)}, u32[]{:S(2)}, u32[]{:S(2)}) async-start(bf16[128,9,2,128]{3,2,1,0:T(2,128)(2,1)} %bitcast.10), calls=%async_computation.1 | async-start | bytes 1179648 | tf_op jit(solution)/shard_map/all_to_all | solution.py:239
  46.1 26.0 %copy-start.1 = (f32[4096]{0:T(1024)S(1)}, f32[4096]{0:T(1024)}, u32[]{:S(2)}) copy-start(f32[4096]{0:T(1024)} %param.11) | copy-start | bytes 49156
  46.1 26.0 %copy-start.2 = (s32[16,3]{0,1:T(4,128)S(1)}, s32[16,3]{0,1:T(4,128)}, u32[]{:S(2)}) copy-start(s32[16,3]{0,1:T(4,128)} %param.8) | copy-start | bytes 580
  46.1 26.0 %copy-start.3 = (f32[2]{0:T(128)S(1)}, f32[2]{0:T(128)}, u32[]{:S(2)}) copy-start(f32[2]{0:T(128)} %pair_energy_ref.1) | copy-start | bytes 28
  46.2 16.9 %collective-permute-start = (bf16[384,384]{1,0:T(8,128)(2,1)S(1)}, bf16[384,384]{1,0:T(8,128)(2,1)S(1)}, u32[]{:S(2)}, u32[]{:S(2)}) collective-permute-start(bf16[384,384]{1,0:T(8,128)(2,1)S(1)} %dynamic-slice_bitcast_fusion), channel_id=1, source_target_pairs={{256,0},{384,128},{0,256},{128,384},{257,1},{385,129},{1,257},{129... | collective-permute-start | bytes 884744 | tf_op jit(solution)/shard_map/ppermute | solution.py:222
  70.2 10.1 %collective-permute-start.2 = (bf16[384,384]{1,0:T(8,128)(2,1)S(1)}, bf16[384,384]{1,0:T(8,128)(2,1)S(1)}, u32[]{:S(2)}, u32[]{:S(2)}) collective-permute-start(bf16[384,384]{1,0:T(8,128)(2,1)S(1)} %get-tuple-element.9), channel_id=1, source_target_pairs={{256,0},{384,128},{0,256},{128,384},{257,1},{385,129},{1,257},{129... | collective-permute-start | bytes 884744 | tf_op jit(solution)/shard_map/ppermute | solution.py:253

commit v3 on v2

--- a/solution.py
+++ b/solution.py
@@ -57,19 +57,26 @@
         out_ref[u] = packed
 
 
-def select_kernel(info_ref, mine_ref, theirs_ref, out_ref, wide, staged, tile_rows, tiles, sem):
-    slab = ROWS * MSG1
-    core = info_ref[1]
-    start = pl.multiple_of(info_ref[0] * slab, 16)
+def scalar_of(row):
+    return jnp.max(row).astype(jnp.int32)
+
+
+def table_kernel(place_ref, held_ref, out_ref):
+    start = pl.multiple_of(scalar_of(place_ref[0:1]) * (ROWS * MSG1), 16)
+    for group in range(GROUP // 2):
+        row = group * MSG1 + NT
+        block = held_ref[pl.ds(pl.multiple_of(start + row // 16 * 16, 16), 16), :].astype(jnp.float32)
+        named = block[row % 16 : row % 16 + 1].astype(jnp.int32)
+        strip = ((named >> 2) & 1) * ROWS + (named >> 3) * NB + (named & (NB - 1))
+        out_ref[pl.ds(group, 1), :] = 2 * named
+        out_ref[pl.ds(GROUP // 2 + group, 1), :] = 2 * MSG1 * strip
+
+
+def select_kernel(place_ref, table_ref, mine_ref, theirs_ref, out_ref, wide, staged, table, sem):
+    copy = pltpu.make_async_copy(table_ref, table, sem)
+    copy.start()
+    core = scalar_of(place_ref[1:2])
     wide[pl.ds(core, HELD, stride=2), :] = mine_ref[...].astype(jnp.float32)
-    first = 2 * (start + NT) + core
-    for group in range(GROUP // 2):
-        named = wide[pl.ds(first + 2 * group * MSG1, 1), :].astype(jnp.int32)
-        tile_rows[pl.ds(group, 1), :] = 2 * named
-        place = ((named >> 2) & 1) * ROWS + (named >> 3) * NB + (named & (NB - 1))
-        tile_rows[pl.ds(GROUP // 2 + group, 1), :] = 2 * MSG1 * place
-    copy = pltpu.make_async_copy(tile_rows, tiles, sem)
-    copy.start()
     wide[pl.ds(1 - core, HELD, stride=2), :] = theirs_ref[...].astype(jnp.float32)
     copy.wait()
 
@@ -77,8 +84,8 @@
         for parity in range(2):
             for y in range(NY):
                 lanes = [(2 * y + parity) * K + k for k in range(K)]
-                named = [tiles[group, lane] for lane in lanes]
-                strips = [tiles[GROUP // 2 + group, lane] for lane in lanes]
+                named = [table[group, lane] for lane in lanes]
+                strips = [table[GROUP // 2 + group, lane] for lane in lanes]
                 base = group * MSG2 + (y * ROWS + parity * (GROUP // 2)) * MSG2
                 for l in range(K):
                     for k in range(K):
@@ -94,7 +101,7 @@
 ACROSS = (((1,), (1,)), ((), ()))
 
 
-def ladder_kernel(info_ref, amps_ref, mirror_amps_ref, blocks_ref, sent_ref, domain, half, mirror_half, wide):
+def ladder_kernel(place_ref, amps_ref, mirror_amps_ref, blocks_ref, sent_ref, domain, half, mirror_half, wide):
     wide[...] = blocks_ref[...].astype(jnp.float32)
     left = lax.broadcasted_iota(jnp.int32, (ROWS, V), 1) < HALF
     for y in range(NY):
@@ -110,15 +117,13 @@
                         sides[1] if q == 1 else pltpu.roll(sides[1], HALF, 1),
                     )
                     domain[rows, pl.ds(q * WIDTH + l * V, V)] = block.astype(jnp.bfloat16)
-    own = amps_ref[info_ref[2]]
-    mirrored = mirror_amps_ref[...]
+    own = amps_ref[scalar_of(place_ref[2:3])]
+    both = jnp.concatenate([own, mirror_amps_ref[...]], axis=1)
     for q in range(NQ):
         columns = pl.ds(q * WIDTH, WIDTH)
-        part = domain[:, columns]
-        half[:, columns] = jnp.dot(part, own, preferred_element_type=jnp.float32).astype(jnp.bfloat16)
-        mirror_half[:, columns] = jnp.dot(part, mirrored, preferred_element_type=jnp.float32).astype(
-            jnp.bfloat16
-        )
+        halves = jnp.dot(domain[:, columns], both, preferred_element_type=jnp.float32).astype(jnp.bfloat16)
+        half[:, columns] = halves[:, :WIDTH]
+        mirror_half[:, columns] = halves[:, WIDTH:]
     sent_ref[...] = (
         lax.dot_general(domain[...], half[...], ACROSS, preferred_element_type=jnp.float32)
         + lax.dot_general(mirror_half[...], domain[...], ACROSS, preferred_element_type=jnp.float32)
@@ -178,11 +183,11 @@
 
 
 def other_kernel(
-    info_ref, amps_ref, received_ref, denominators_ref, residual_in, updated_in,
+    place_ref, amps_ref, received_ref, denominators_ref, residual_in, updated_in,
     residual_out, updated_out, residual_buf, updated_buf, sems,
 ):
     write_pair(
-        1 - info_ref[2],
+        1 - scalar_of(place_ref[2:3]),
         lambda step: denominators_ref[pl.ds(step * V, V), :],
         lambda band: received_ref[band, :].astype(jnp.float32),
         amps_ref, residual_out, updated_out, residual_buf, updated_buf, sems,
@@ -198,6 +203,7 @@
     x = lax.axis_index("x")
     sel = jnp.where(x < NX // 2, 0, 1 - (mirror[0] & 1))
     info = jnp.stack([lax.axis_index(a) for a in ("u", "c")] + [sel, lax.axis_index("y")]).astype(jnp.int32)
+    place = jnp.broadcast_to(info.astype(f32)[:, None], (4, V))
     tiles_t = tiles.T
 
     spread = pl.pallas_call(
@@ -221,21 +227,30 @@
     opposite = [((i + NX // 2) % NX, i) for i in range(NX)]
     mirror_amps = lax.ppermute(going, "x", opposite)
 
+    held = held.reshape(HELD, V)
+    table = pl.pallas_call(
+        table_kernel,
+        out_shape=jax.ShapeDtypeStruct((GROUP, V), jnp.int32),
+        in_specs=[whole(), whole()],
+        out_specs=whole(),
+        compiler_params=PARAMS,
+        name="table",
+    )(place, held)
     selected = pl.pallas_call(
         select_kernel,
         out_shape=jax.ShapeDtypeStruct((PLANE * MSG2, V), bf16),
-        in_specs=[whole(SMEM), whole(), whole()],
+        in_specs=[whole()] * 4,
         out_specs=whole(),
         scratch_shapes=[
             pltpu.VMEM((NC * HELD, V), f32),
             pltpu.VMEM((PLANE * MSG2, V), f32),
-            pltpu.VMEM((GROUP, V), jnp.int32),
             pltpu.SMEM((GROUP, V), jnp.int32),
             pltpu.SemaphoreType.DMA,
         ],
         compiler_params=PARAMS,
         name="select",
-    )(info, held.reshape(HELD, V), theirs.reshape(HELD, V))
+    )(place, table, held, theirs.reshape(HELD, V))
+    selected, mirror_amps = lax.optimization_barrier((selected, mirror_amps))
     blocks = lax.all_to_all(
         selected.reshape(PLANE, MSG2 // 2, 2, V), ("y", "x", "b"), 0, 0, tiled=True
     )
@@ -244,12 +259,12 @@
     sent, domain, half, mirror_half = pl.pallas_call(
         ladder_kernel,
         out_shape=(jax.ShapeDtypeStruct((WIDTH, WIDTH), bf16), wide_half, wide_half, wide_half),
-        in_specs=[whole(SMEM), whole(), whole(), whole()],
+        in_specs=[whole()] * 4,
         out_specs=(whole(),) * 4,
         scratch_shapes=[pltpu.VMEM((PLANE * MSG2, V), f32)],
         compiler_params=PARAMS,
         name="ladder",
-    )(info, amplitudes, mirror_amps, blocks.reshape(PLANE * MSG2, V))
+    )(place, amplitudes, mirror_amps, blocks.reshape(PLANE * MSG2, V))
     received = lax.ppermute(sent, "x", opposite)
 
     energies = virt_energy.reshape(NT, V)
@@ -275,14 +290,14 @@
     residual, updated = pl.pallas_call(
         other_kernel,
         out_shape=outs,
-        in_specs=[whole(SMEM), whole(), whole(), whole(), whole(pl.ANY), whole(pl.ANY)],
+        in_specs=[whole(), whole(), whole(), whole(), whole(pl.ANY), whole(pl.ANY)],
         out_specs=(whole(pl.ANY),) * 2,
         scratch_shapes=buffers,
         input_output_aliases={4: 0, 5: 1},
         cost_estimate=pl.CostEstimate(flops=4 * WIDTH**2, bytes_accessed=10 * WIDTH**2, transcendentals=0),
         compiler_params=PARAMS,
         name="other",
-    )(info, amplitudes, received, denominators, residual, updated)
+    )(place, amplitudes, received, denominators, residual, updated)
     return (residual, updated)
 
 

time: 82.2 us -> 79.8 us (0.971)
  waiting for transfers between devices: 23.3 us -> 15 us
  blocking collectives: 27.1 us -> 31.5 us
  starting transfers between devices: 18.5 us -> 22.2 us
  Pallas kernels: 11.3 us -> 9.05 us
    ppermute x1, waiting for transfers between devices: 12 us -> 0.01 us  [shards(): mirror_amps = lax.ppermute(going, 'x', opposite)]
    all_to_all x1, blocking collectives: 27.1 us -> 31.5 us  [shards(): lax.all_to_all(selected.reshape(PLANE, MSG2 // 2, 2, V), ('y', 'x', 'b'),...]
    all_to_all x1, starting transfers between devices: 9.78 us -> 13.2 us  [shards(): lax.all_to_all(spread.reshape(SOURCES, MSG1 // 2, 2, V), ('u', 'x', 'b'),...]
    all_to_all x1, waiting for transfers between devices: 4.91 us -> 8.09 us  [shards(): lax.all_to_all(spread.reshape(SOURCES, MSG1 // 2, 2, V), ('u', 'x', 'b'),...]
    pallas_call x1, Pallas kernels: 3.21 us -> 1.79 us  [shards(): pl.pallas_call(select_kernel, out_shape=jax.ShapeDtypeStruct((PLANE * MSG...]
  transfers between devices with their start and end apart: 4 -> 4, of which waited for: 4 -> 3; matrix products, arithmetic and copies ran while one was open for 0% -> 0% of each run, Pallas kernels for 3% -> 6%
where the time goes in v3:
time: 79.8 us; the launch traced here: 79.4 us
  blocking collectives  31.5 us (39%)
  starting transfers between devices  22.2 us (28%)
  waiting for transfers between devices  15 us (19%)
  Pallas kernels  9.05 us (11%)
  between operations  1.45 us (2%)
    all_to_all x1, blocking collectives, shards(): lax.all_to_all(selected.reshape(PLANE, MSG2 // 2, 2, V), ('y', 'x', 'b'),...  31.5 us
    all_to_all x1, starting transfers between devices, shards(): lax.all_to_all(spread.reshape(SOURCES, MSG1 // 2, 2, V), ('u', 'x', 'b'),...  13.2 us
    all_to_all x1, waiting for transfers between devices, shards(): lax.all_to_all(spread.reshape(SOURCES, MSG1 // 2, 2, V), ('u', 'x', 'b'),...  8.09 us
    ppermute x1, waiting for transfers between devices, shards(): received = lax.ppermute(sent, 'x', opposite)  5.65 us
    ppermute x1, starting transfers between devices, shards(): mirror_amps = lax.ppermute(going, 'x', opposite)  5.21 us
    pallas_call x1, Pallas kernels, shards(): pl.pallas_call(own_kernel, out_shape=outs + (jax.ShapeDtypeStruct((WIDTH,...  2.5 us
    pallas_call x1, Pallas kernels, shards(): pl.pallas_call(spread_kernel, out_shape=jax.ShapeDtypeStruct((NU, ROWS *...  1.96 us
    ppermute x1, starting transfers between devices, shards(): received = lax.ppermute(sent, 'x', opposite)  1.93 us
  transfers between devices with their start and end apart: 4, of which 3 were waited for; matrix products, arithmetic and copies ran while one was open for 0% of the time, Pallas kernels for 6%

profile of v3, /device:TPU:8, one launch (start us, length us, event | category | flops | bytes accessed | tf_op | source)
XLA Modules:
  0.0 79.4 jit_solution(11765879481052561491)
XLA Ops:
  0.6 0.0 copy-start
  0.6 2.0 %spread.1 = bf16[2,544,128]{2,1,0:T(8,128)(2,1)} custom-call(s32[3,16]{1,0:T(4,128)} %bitcast.21, bf16[2,32,16,64]{3,2,1,0:T(8,128)(2,1)} %factors_hbm.1), custom_call_target="tpu_custom_call" | custom-call | tf_op jit(solution)/shard_map/spread/pallas_call | solution.py:209
  2.6 13.2 %all-to-all-start = ((bf16[32,17,2,128]{3,2,1,0:T(2,128)(2,1)}), bf16[32,17,2,128]{3,2,1,0:T(2,128)(2,1)S(1)}, u32[]{:S(2)}, u32[]{:S(2)}) async-start(bf16[32,17,2,128]{3,2,1,0:T(2,128)(2,1)} %bitcast.23), calls=%async_computation | async-start | bytes 557056 | tf_op jit(solution)/shard_map/all_to_all | solution.py:224
  16.5 0.0 copy-done
  16.5 5.2 %collective-permute-start.1 = (bf16[384,384]{1,0:T(8,128)(2,1)S(1)}, bf16[384,384]{1,0:T(8,128)(2,1)S(1)}, u32[]{:S(2)}, u32[]{:S(2)}) collective-permute-start(bf16[384,384]{1,0:T(8,128)(2,1)S(1)} %dynamic-slice_bitcast_fusion), channel_id=1, source_target_pairs={{256,0},{384,128},{0,256},{128,384},{257,1},{385,129},{1,257},{129... | collective-permute-start | bytes 884744 | tf_op jit(solution)/shard_map/ppermute | solution.py:228
  21.7 8.1 %all-to-all-done = bf16[32,17,2,128]{3,2,1,0:T(2,128)(2,1)S(1)} async-done(((bf16[32,17,2,128]{3,2,1,0:T(2,128)(2,1)}), bf16[32,17,2,128]{3,2,1,0:T(2,128)(2,1)S(1)}, u32[]{:S(2)}, u32[]{:S(2)}) %all-to-all-start) | async-done | bytes 278560 | tf_op jit(solution)/shard_map/all_to_all | solution.py:224
  29.8 1.9 %collective-permute-start = (bf16[32,17,2,128]{3,2,1,0:T(2,128)(2,1)S(1)}, bf16[32,17,2,128]{3,2,1,0:T(2,128)(2,1)S(1)}, u32[]{:S(2)}, u32[]{:S(2)}) collective-permute-start(bf16[32,17,2,128]{3,2,1,0:T(2,128)(2,1)S(1)} %all-to-all-done), channel_id=1, source_target_pairs={{8,0},{0,8},{9,1},{1,9},{10,2},{2,10},{11,3},{3,11},{12,4},{4,12},... | collective-permute-start | bytes 835592 | tf_op jit(solution)/shard_map/ppermute | solution.py:225
  31.7 0.1 fusion
  31.8 0.1 broadcast_in_dim.2.place_ref
  31.9 0.1 table.1.table_ref
  32.0 1.2 %collective-permute-done = bf16[32,17,2,128]{3,2,1,0:T(2,128)(2,1)S(1)} collective-permute-done((bf16[32,17,2,128]{3,2,1,0:T(2,128)(2,1)S(1)}, bf16[32,17,2,128]{3,2,1,0:T(2,128)(2,1)S(1)}, u32[]{:S(2)}, u32[]{:S(2)}) %collective-permute-start) | collective-permute-done | bytes 278560 | tf_op jit(solution)/shard_map/ppermute | solution.py:225
  33.3 1.8 %select.1 = bf16[2304,128]{1,0:T(8,128)(2,1)S(1)} custom-call(f32[4,128]{1,0:T(4,128)S(1)} %broadcast_in_dim.2.place_ref, s32[16,128]{1,0:T(8,128)S(1)} %table.1.table_ref, bf16[1088,128]{1,0:T(8,128)(2,1)S(1)} %bitcast.16, bf16[1088,128]{1,0:T(8,128)(2,1)S(1)} %bitcast.19), custom_call_target="tpu_custom_call" | custom-call | tf_op jit(solution)/shard_map/select/pallas_call | solution.py:239
  35.1 0.0 collective-permute-done.1.mirror_amps_ref
  35.1 0.0 copy-start.1
  35.1 0.0 copy-start.2
  35.1 0.0 copy-start.3
  35.1 31.5 %all_to_all.10 = bf16[128,9,2,128]{3,2,1,0:T(2,128)(2,1)S(1)} all-to-all(bf16[128,9,2,128]{3,2,1,0:T(2,128)(2,1)S(1)} %bitcast.17), channel_id=1, replica_groups=mesh['x'=4,'u'=2,'b'=4,'c'=2,'y'=8] {'y','x','b'}, dimensions={0} | all-to-all | bytes 1179648 | tf_op jit(solution)/shard_map/all_to_all | solution.py:254
  66.6 1.6 %ladder.1 = (bf16[384,384]{1,0:T(8,128)(2,1)S(1)}, bf16[384,768]{1,0:T(8,128)(2,1)S(1)}, bf16[384,768]{1,0:T(8,128)(2,1)S(1)}, bf16[384,768]{1,0:T(8,128)(2,1)S(1)}) custom-call(f32[4,128]{1,0:T(4,128)S(1)} %broadcast_in_dim.2.place_ref, bf16[2,384,384]{2,1,0:T(8,128)(2,1)S(1)} %copy-done, bf16[384,384]{1,0:T(8,128)(2,1)S(1)} %collective-permute-done.1.mirror_amps_ref, ...), custom_call_target="tpu_custom_call" | custom-call | tf_op jit(solution)/shard_map/ladder/pallas_call | solution.py:259
  68.2 1.9 %collective-permute-start.2 = (bf16[384,384]{1,0:T(8,128)(2,1)S(1)}, bf16[384,384]{1,0:T(8,128)(2,1)S(1)}, u32[]{:S(2)}, u32[]{:S(2)}) collective-permute-start(bf16[384,384]{1,0:T(8,128)(2,1)S(1)} %get-tuple-element.13), channel_id=1, source_target_pairs={{256,0},{384,128},{0,256},{128,384},{257,1},{385,129},{1,257},{129... | collective-permute-start | bytes 884744 | tf_op jit(solution)/shard_map/ppermute | solution.py:268
  70.2 0.0 copy-done.1
  70.2 0.0 copy-done.2
  70.2 0.0 copy-done.3
  70.2 2.5 %own.1 = (f32[2,384,384]{2,1,0:T(8,128)}, bf16[2,384,384]{2,1,0:T(8,128)(2,1)}, f32[384,384]{1,0:T(8,128)S(1)}) custom-call(s32[4]{0:T(128)S(1)} %get-tuple-element.21.info_ref, s32[3,16]{1,0:T(4,128)S(1)} %bitcast.22, f32[2]{0:T(128)S(1)} %copy-done.3, f32[32,128]{1,0:T(8,128)S(1)} %bitcast.20, bf16[2,384,384]{2,1,0:T(8,128)(2,1)S(1)} %copy-done, ...), custom_call_target="tpu_custom_call" | custom-call | flops 452984832 | bytes 1474560 | tf_op jit(solution)/shard_map/own/pallas_call | solution.py:280
  72.7 5.6 %collective-permute-done.2.received_ref = bf16[384,384]{1,0:T(8,128)(2,1)S(1)} collective-permute-done((bf16[384,384]{1,0:T(8,128)(2,1)S(1)}, bf16[384,384]{1,0:T(8,128)(2,1)S(1)}, u32[]{:S(2)}, u32[]{:S(2)}) %collective-permute-start.2) | collective-permute-done | bytes 294944 | tf_op jit(solution)/shard_map/ppermute | solution.py:268
  78.3 1.1 %other.1 = (f32[2,384,384]{2,1,0:T(8,128)}, bf16[2,384,384]{2,1,0:T(8,128)(2,1)}) custom-call(f32[4,128]{1,0:T(4,128)S(1)} %broadcast_in_dim.2.place_ref, bf16[2,384,384]{2,1,0:T(8,128)(2,1)S(1)} %copy-done, bf16[384,384]{1,0:T(8,128)(2,1)S(1)} %collective-permute-done.2.received_ref, ...), custom_call_target="tpu_custom_call", output_to_operand_aliasing={{0}: (4, {}), {1}: (5, {})} | custom-call | flops 589824 | bytes 1474560 | tf_op jit(solution)/shard_map/other/pallas_call | solution.py:290
  (1 shorter events, 0.0 us)
Async XLA Ops:
  0.6 15.8 %copy-start = (bf16[2,384,384]{2,1,0:T(8,128)(2,1)S(1)}, bf16[2,384,384]{2,1,0:T(8,128)(2,1)}, u32[]{:S(2)}) copy-start(bf16[2,384,384]{2,1,0:T(8,128)(2,1)} %amps_ref.5) | copy-start | bytes 1769476
  2.6 27.2 %all-to-all-start = ((bf16[32,17,2,128]{3,2,1,0:T(2,128)(2,1)}), bf16[32,17,2,128]{3,2,1,0:T(2,128)(2,1)S(1)}, u32[]{:S(2)}, u32[]{:S(2)}) async-start(bf16[32,17,2,128]{3,2,1,0:T(2,128)(2,1)} %bitcast.23), calls=%async_computation | async-start | bytes 557056 | tf_op jit(solution)/shard_map/all_to_all | solution.py:224
  16.5 18.6 %collective-permute-start.1 = (bf16[384,384]{1,0:T(8,128)(2,1)S(1)}, bf16[384,384]{1,0:T(8,128)(2,1)S(1)}, u32[]{:S(2)}, u32[]{:S(2)}) collective-permute-start(bf16[384,384]{1,0:T(8,128)(2,1)S(1)} %dynamic-slice_bitcast_fusion), channel_id=1, source_target_pairs={{256,0},{384,128},{0,256},{128,384},{257,1},{385,129},{1,257},{129... | collective-permute-start | bytes 884744 | tf_op jit(solution)/shard_map/ppermute | solution.py:228
  29.8 3.4 %collective-permute-start = (bf16[32,17,2,128]{3,2,1,0:T(2,128)(2,1)S(1)}, bf16[32,17,2,128]{3,2,1,0:T(2,128)(2,1)S(1)}, u32[]{:S(2)}, u32[]{:S(2)}) collective-permute-start(bf16[32,17,2,128]{3,2,1,0:T(2,128)(2,1)S(1)} %all-to-all-done), channel_id=1, source_target_pairs={{8,0},{0,8},{9,1},{1,9},{10,2},{2,10},{11,3},{3,11},{12,4},{4,12},... | collective-permute-start | bytes 835592 | tf_op jit(solution)/shard_map/ppermute | solution.py:225
  35.1 35.1 %copy-start.1 = (f32[4096]{0:T(1024)S(1)}, f32[4096]{0:T(1024)}, u32[]{:S(2)}) copy-start(f32[4096]{0:T(1024)} %param.11) | copy-start | bytes 49156
  35.1 35.1 %copy-start.2 = (s32[16,3]{0,1:T(4,128)S(1)}, s32[16,3]{0,1:T(4,128)}, u32[]{:S(2)}) copy-start(s32[16,3]{0,1:T(4,128)} %param.8) | copy-start | bytes 580
  35.1 35.1 %copy-start.3 = (f32[2]{0:T(128)S(1)}, f32[2]{0:T(128)}, u32[]{:S(2)}) copy-start(f32[2]{0:T(128)} %pair_energy_ref.1) | copy-start | bytes 28
  68.2 10.1 %collective-permute-start.2 = (bf16[384,384]{1,0:T(8,128)(2,1)S(1)}, bf16[384,384]{1,0:T(8,128)(2,1)S(1)}, u32[]{:S(2)}, u32[]{:S(2)}) collective-permute-start(bf16[384,384]{1,0:T(8,128)(2,1)S(1)} %get-tuple-element.13), channel_id=1, source_target_pairs={{256,0},{384,128},{0,256},{128,384},{257,1},{385,129},{1,257},{129... | collective-permute-start | bytes 884744 | tf_op jit(solution)/shard_map/ppermute | solution.py:268

commit v4 on v3

--- a/solution.py
+++ b/solution.py
@@ -25,6 +25,7 @@
 
 
 def spread_kernel(tiles_hbm, factors_hbm, out_ref, tiles, raw, wide, staged, sems):
+    slots = [(row % NB) * NX + row // NB for row in range(ROWS)]
     copies = [pltpu.make_async_copy(tiles_hbm, tiles, sems.at[0])]
     part = NT // 2
     for i in range(2):
@@ -39,7 +40,7 @@
         for k in range(K):
             tile_row = jnp.where(lane == member * K + k, tiles[k, member].astype(jnp.float32), tile_row)
     for row in range(ROWS):
-        staged[pl.ds(row * MSG1 + NT, 2), :] = tile_row
+        staged[pl.ds(slots[row] * MSG1 + NT, 2), :] = tile_row
     for i in range(2):
         copies[1 + i].wait()
         for q in range(NQ):
@@ -51,7 +52,7 @@
             for eight in range(part // 8):
                 first = (i * part + eight * 8) * ROWS + row
                 sides = [wide[pl.ds(q * NT * ROWS + first, 8, stride=ROWS), :] for q in range(NQ)]
-                staged[pl.ds(row * MSG1 + i * part + eight * 8, 8), :] = jnp.concatenate(sides, axis=1)
+                staged[pl.ds(slots[row] * MSG1 + i * part + eight * 8, 8), :] = jnp.concatenate(sides, axis=1)
     packed = staged[...].astype(jnp.bfloat16)
     for u in range(NU):
         out_ref[u] = packed
@@ -64,10 +65,10 @@
 def table_kernel(place_ref, held_ref, out_ref):
     start = pl.multiple_of(scalar_of(place_ref[0:1]) * (ROWS * MSG1), 16)
     for group in range(GROUP // 2):
-        row = group * MSG1 + NT
+        row = (group % NB * NX + group // NB) * MSG1 + NT
         block = held_ref[pl.ds(pl.multiple_of(start + row // 16 * 16, 16), 16), :].astype(jnp.float32)
         named = block[row % 16 : row % 16 + 1].astype(jnp.int32)
-        strip = ((named >> 2) & 1) * ROWS + (named >> 3) * NB + (named & (NB - 1))
+        strip = ((named >> 2) & 1) * ROWS + (named & (NB - 1)) * NX + (named >> 3)
         out_ref[pl.ds(group, 1), :] = 2 * named
         out_ref[pl.ds(GROUP // 2 + group, 1), :] = 2 * MSG1 * strip
 
@@ -81,12 +82,13 @@
     copy.wait()
 
     def one_group(group, carry):
+        first = (group // NB * (NY * NB) + group % NB) * MSG2
         for parity in range(2):
             for y in range(NY):
                 lanes = [(2 * y + parity) * K + k for k in range(K)]
                 named = [table[group, lane] for lane in lanes]
                 strips = [table[GROUP // 2 + group, lane] for lane in lanes]
-                base = group * MSG2 + (y * ROWS + parity * (GROUP // 2)) * MSG2
+                base = first + (parity * (NX // 2) * NY + y) * NB * MSG2
                 for l in range(K):
                     for k in range(K):
                         staged[pl.ds(base + (l * K + k) * 2, 2), :] = wide[
@@ -102,7 +104,12 @@
 
 
 def ladder_kernel(place_ref, amps_ref, mirror_amps_ref, blocks_ref, sent_ref, domain, half, mirror_half, wide):
-    wide[...] = blocks_ref[...].astype(jnp.float32)
+    run = NB * MSG2
+    for x in range(NX):
+        for y in range(0, NY, 2):
+            chunk = blocks_ref[pl.ds((x * NY + y) * run, 2 * run), :].astype(jnp.float32)
+            wide[pl.ds((y * NX + x) * run, run), :] = chunk[:run]
+            wide[pl.ds(((y + 1) * NX + x) * run, run), :] = chunk[run:]
     left = lax.broadcasted_iota(jnp.int32, (ROWS, V), 1) < HALF
     for y in range(NY):
         for l in range(K):
@@ -221,7 +228,7 @@
         compiler_params=pltpu.CompilerParams(vmem_limit_bytes=60 * 1024 * 1024),
         name="spread",
     )(tiles_t, factors)
-    held = lax.all_to_all(spread.reshape(SOURCES, MSG1 // 2, 2, V), ("u", "x", "b"), 0, 0, tiled=True)
+    held = lax.all_to_all(spread.reshape(SOURCES, MSG1 // 2, 2, V), ("u", "b", "x"), 0, 0, tiled=True)
     theirs = lax.ppermute(held, "c", [(1, 0), (0, 1)])
     going = lax.dynamic_index_in_dim(amplitudes, 1 - sel, 0, keepdims=False)
     opposite = [((i + NX // 2) % NX, i) for i in range(NX)]
@@ -252,7 +259,7 @@
     )(place, table, held, theirs.reshape(HELD, V))
     selected, mirror_amps = lax.optimization_barrier((selected, mirror_amps))
     blocks = lax.all_to_all(
-        selected.reshape(PLANE, MSG2 // 2, 2, V), ("y", "x", "b"), 0, 0, tiled=True
+        selected.reshape(PLANE, MSG2 // 2, 2, V), ("x", "y", "b"), 0, 0, tiled=True
     )
 
     wide_half = jax.ShapeDtypeStruct((WIDTH, NQ * WIDTH), bf16)

time: 79.8 us -> 78.7 us (0.986)
  the two profiles are of different devices: /device:TPU:8 before, /device:TPU:16 now
where the time goes in v4:
time: 78.7 us; the launch traced here: 78.3 us
  blocking collectives  31.1 us (40%)
  starting transfers between devices  23 us (29%)
  waiting for transfers between devices  13.5 us (17%)
  Pallas kernels  9.08 us (12%)
  between operations  1.45 us (2%)
    all_to_all x1, blocking collectives, shards(): lax.all_to_all(selected.reshape(PLANE, MSG2 // 2, 2, V), ('x', 'y', 'b'),...  31.1 us
    all_to_all x1, starting transfers between devices, shards(): lax.all_to_all(spread.reshape(SOURCES, MSG1 // 2, 2, V), ('u', 'b', 'x'),...  13.2 us
    all_to_all x1, waiting for transfers between devices, shards(): lax.all_to_all(spread.reshape(SOURCES, MSG1 // 2, 2, V), ('u', 'b', 'x'),...  7.19 us
    ppermute x1, starting transfers between devices, shards(): mirror_amps = lax.ppermute(going, 'x', opposite)  5.2 us
    ppermute x1, waiting for transfers between devices, shards(): received = lax.ppermute(sent, 'x', opposite)  5.06 us
    ppermute x1, starting transfers between devices, shards(): received = lax.ppermute(sent, 'x', opposite)  2.72 us
    pallas_call x1, Pallas kernels, shards(): pl.pallas_call(own_kernel, out_shape=outs + (jax.ShapeDtypeStruct((WIDTH,...  2.51 us
    pallas_call x1, Pallas kernels, shards(): pl.pallas_call(spread_kernel, out_shape=jax.ShapeDtypeStruct((NU, ROWS *...  1.96 us
  transfers between devices with their start and end apart: 4, of which 3 were waited for; matrix products, arithmetic and copies ran while one was open for 0% of the time, Pallas kernels for 6%

profile of v4, /device:TPU:16, one launch (start us, length us, event | category | flops | bytes accessed | tf_op | source)
XLA Modules:
  0.0 78.3 jit_solution(1520946407040977702)
XLA Ops:
  0.6 0.0 copy-start
  0.6 2.0 %spread.1 = bf16[2,544,128]{2,1,0:T(8,128)(2,1)} custom-call(s32[3,16]{1,0:T(4,128)} %bitcast.21, bf16[2,32,16,64]{3,2,1,0:T(8,128)(2,1)} %factors_hbm.1), custom_call_target="tpu_custom_call" | custom-call | tf_op jit(solution)/shard_map/spread/pallas_call | solution.py:216
  2.6 13.2 %all-to-all-start = ((bf16[32,17,2,128]{3,2,1,0:T(2,128)(2,1)}), bf16[32,17,2,128]{3,2,1,0:T(2,128)(2,1)S(1)}, u32[]{:S(2)}, u32[]{:S(2)}) async-start(bf16[32,17,2,128]{3,2,1,0:T(2,128)(2,1)} %bitcast.23), calls=%async_computation | async-start | bytes 557056 | tf_op jit(solution)/shard_map/all_to_all | solution.py:231
  16.5 0.0 copy-done
  16.5 5.2 %collective-permute-start.1 = (bf16[384,384]{1,0:T(8,128)(2,1)S(1)}, bf16[384,384]{1,0:T(8,128)(2,1)S(1)}, u32[]{:S(2)}, u32[]{:S(2)}) collective-permute-start(bf16[384,384]{1,0:T(8,128)(2,1)S(1)} %dynamic-slice_bitcast_fusion), channel_id=1, source_target_pairs={{256,0},{384,128},{0,256},{128,384},{257,1},{385,129},{1,257},{129... | collective-permute-start | bytes 884744 | tf_op jit(solution)/shard_map/ppermute | solution.py:235
  21.7 7.2 %all-to-all-done = bf16[32,17,2,128]{3,2,1,0:T(2,128)(2,1)S(1)} async-done(((bf16[32,17,2,128]{3,2,1,0:T(2,128)(2,1)}), bf16[32,17,2,128]{3,2,1,0:T(2,128)(2,1)S(1)}, u32[]{:S(2)}, u32[]{:S(2)}) %all-to-all-start) | async-done | bytes 278560 | tf_op jit(solution)/shard_map/all_to_all | solution.py:231
  28.9 1.9 %collective-permute-start = (bf16[32,17,2,128]{3,2,1,0:T(2,128)(2,1)S(1)}, bf16[32,17,2,128]{3,2,1,0:T(2,128)(2,1)S(1)}, u32[]{:S(2)}, u32[]{:S(2)}) collective-permute-start(bf16[32,17,2,128]{3,2,1,0:T(2,128)(2,1)S(1)} %all-to-all-done), channel_id=1, source_target_pairs={{8,0},{0,8},{9,1},{1,9},{10,2},{2,10},{11,3},{3,11},{12,4},{4,12},... | collective-permute-start | bytes 835592 | tf_op jit(solution)/shard_map/ppermute | solution.py:232
  30.8 0.1 fusion
  30.9 0.1 broadcast_in_dim.2.place_ref
  31.0 0.1 table.1.table_ref
  31.1 1.2 %collective-permute-done = bf16[32,17,2,128]{3,2,1,0:T(2,128)(2,1)S(1)} collective-permute-done((bf16[32,17,2,128]{3,2,1,0:T(2,128)(2,1)S(1)}, bf16[32,17,2,128]{3,2,1,0:T(2,128)(2,1)S(1)}, u32[]{:S(2)}, u32[]{:S(2)}) %collective-permute-start) | collective-permute-done | bytes 278560 | tf_op jit(solution)/shard_map/ppermute | solution.py:232
  32.3 1.8 %select.1 = bf16[2304,128]{1,0:T(8,128)(2,1)S(1)} custom-call(f32[4,128]{1,0:T(4,128)S(1)} %broadcast_in_dim.2.place_ref, s32[16,128]{1,0:T(8,128)S(1)} %table.1.table_ref, bf16[1088,128]{1,0:T(8,128)(2,1)S(1)} %bitcast.16, bf16[1088,128]{1,0:T(8,128)(2,1)S(1)} %bitcast.19), custom_call_target="tpu_custom_call" | custom-call | tf_op jit(solution)/shard_map/select/pallas_call | solution.py:246
  34.2 0.0 collective-permute-done.1.mirror_amps_ref
  34.2 0.0 copy-start.1
  34.2 0.0 copy-start.2
  34.2 0.0 copy-start.3
  34.2 31.1 %all_to_all.10 = bf16[128,9,2,128]{3,2,1,0:T(2,128)(2,1)S(1)} all-to-all(bf16[128,9,2,128]{3,2,1,0:T(2,128)(2,1)S(1)} %bitcast.17), channel_id=1, replica_groups=mesh['x'=4,'u'=2,'b'=4,'c'=2,'y'=8] {'x','y','b'}, dimensions={0} | all-to-all | bytes 1179648 | tf_op jit(solution)/shard_map/all_to_all | solution.py:261
  65.3 1.6 %ladder.1 = (bf16[384,384]{1,0:T(8,128)(2,1)S(1)}, bf16[384,768]{1,0:T(8,128)(2,1)S(1)}, bf16[384,768]{1,0:T(8,128)(2,1)S(1)}, bf16[384,768]{1,0:T(8,128)(2,1)S(1)}) custom-call(f32[4,128]{1,0:T(4,128)S(1)} %broadcast_in_dim.2.place_ref, bf16[2,384,384]{2,1,0:T(8,128)(2,1)S(1)} %copy-done, bf16[384,384]{1,0:T(8,128)(2,1)S(1)} %collective-permute-done.1.mirror_amps_ref, ...), custom_call_target="tpu_custom_call" | custom-call | tf_op jit(solution)/shard_map/ladder/pallas_call | solution.py:266
  66.9 2.7 %collective-permute-start.2 = (bf16[384,384]{1,0:T(8,128)(2,1)S(1)}, bf16[384,384]{1,0:T(8,128)(2,1)S(1)}, u32[]{:S(2)}, u32[]{:S(2)}) collective-permute-start(bf16[384,384]{1,0:T(8,128)(2,1)S(1)} %get-tuple-element.13), channel_id=1, source_target_pairs={{256,0},{384,128},{0,256},{128,384},{257,1},{385,129},{1,257},{129... | collective-permute-start | bytes 884744 | tf_op jit(solution)/shard_map/ppermute | solution.py:275
  69.6 0.0 copy-done.1
  69.6 0.0 copy-done.2
  69.6 0.0 copy-done.3
  69.7 2.5 %own.1 = (f32[2,384,384]{2,1,0:T(8,128)}, bf16[2,384,384]{2,1,0:T(8,128)(2,1)}, f32[384,384]{1,0:T(8,128)S(1)}) custom-call(s32[4]{0:T(128)S(1)} %get-tuple-element.21.info_ref, s32[3,16]{1,0:T(4,128)S(1)} %bitcast.22, f32[2]{0:T(128)S(1)} %copy-done.3, f32[32,128]{1,0:T(8,128)S(1)} %bitcast.20, bf16[2,384,384]{2,1,0:T(8,128)(2,1)S(1)} %copy-done, ...), custom_call_target="tpu_custom_call" | custom-call | flops 452984832 | bytes 1474560 | tf_op jit(solution)/shard_map/own/pallas_call | solution.py:287
  72.2 5.1 %collective-permute-done.2.received_ref = bf16[384,384]{1,0:T(8,128)(2,1)S(1)} collective-permute-done((bf16[384,384]{1,0:T(8,128)(2,1)S(1)}, bf16[384,384]{1,0:T(8,128)(2,1)S(1)}, u32[]{:S(2)}, u32[]{:S(2)}) %collective-permute-start.2) | collective-permute-done | bytes 294944 | tf_op jit(solution)/shard_map/ppermute | solution.py:275
  77.2 1.1 %other.1 = (f32[2,384,384]{2,1,0:T(8,128)}, bf16[2,384,384]{2,1,0:T(8,128)(2,1)}) custom-call(f32[4,128]{1,0:T(4,128)S(1)} %broadcast_in_dim.2.place_ref, bf16[2,384,384]{2,1,0:T(8,128)(2,1)S(1)} %copy-done, bf16[384,384]{1,0:T(8,128)(2,1)S(1)} %collective-permute-done.2.received_ref, ...), custom_call_target="tpu_custom_call", output_to_operand_aliasing={{0}: (4, {}), {1}: (5, {})} | custom-call | flops 589824 | bytes 1474560 | tf_op jit(solution)/shard_map/other/pallas_call | solution.py:297
  (1 shorter events, 0.0 us)
Async XLA Ops:
  0.6 15.8 %copy-start = (bf16[2,384,384]{2,1,0:T(8,128)(2,1)S(1)}, bf16[2,384,384]{2,1,0:T(8,128)(2,1)}, u32[]{:S(2)}) copy-start(bf16[2,384,384]{2,1,0:T(8,128)(2,1)} %amps_ref.5) | copy-start | bytes 1769476
  2.6 26.3 %all-to-all-start = ((bf16[32,17,2,128]{3,2,1,0:T(2,128)(2,1)}), bf16[32,17,2,128]{3,2,1,0:T(2,128)(2,1)S(1)}, u32[]{:S(2)}, u32[]{:S(2)}) async-start(bf16[32,17,2,128]{3,2,1,0:T(2,128)(2,1)} %bitcast.23), calls=%async_computation | async-start | bytes 557056 | tf_op jit(solution)/shard_map/all_to_all | solution.py:231
  16.5 17.7 %collective-permute-start.1 = (bf16[384,384]{1,0:T(8,128)(2,1)S(1)}, bf16[384,384]{1,0:T(8,128)(2,1)S(1)}, u32[]{:S(2)}, u32[]{:S(2)}) collective-permute-start(bf16[384,384]{1,0:T(8,128)(2,1)S(1)} %dynamic-slice_bitcast_fusion), channel_id=1, source_target_pairs={{256,0},{384,128},{0,256},{128,384},{257,1},{385,129},{1,257},{129... | collective-permute-start | bytes 884744 | tf_op jit(solution)/shard_map/ppermute | solution.py:235
  28.9 3.4 %collective-permute-start = (bf16[32,17,2,128]{3,2,1,0:T(2,128)(2,1)S(1)}, bf16[32,17,2,128]{3,2,1,0:T(2,128)(2,1)S(1)}, u32[]{:S(2)}, u32[]{:S(2)}) collective-permute-start(bf16[32,17,2,128]{3,2,1,0:T(2,128)(2,1)S(1)} %all-to-all-done), channel_id=1, source_target_pairs={{8,0},{0,8},{9,1},{1,9},{10,2},{2,10},{11,3},{3,11},{12,4},{4,12},... | collective-permute-start | bytes 835592 | tf_op jit(solution)/shard_map/ppermute | solution.py:232
  34.2 35.4 %copy-start.1 = (f32[4096]{0:T(1024)S(1)}, f32[4096]{0:T(1024)}, u32[]{:S(2)}) copy-start(f32[4096]{0:T(1024)} %param.11) | copy-start | bytes 49156
  34.2 35.4 %copy-start.2 = (s32[16,3]{0,1:T(4,128)S(1)}, s32[16,3]{0,1:T(4,128)}, u32[]{:S(2)}) copy-start(s32[16,3]{0,1:T(4,128)} %param.8) | copy-start | bytes 580
  34.2 35.4 %copy-start.3 = (f32[2]{0:T(128)S(1)}, f32[2]{0:T(128)}, u32[]{:S(2)}) copy-start(f32[2]{0:T(128)} %pair_energy_ref.1) | copy-start | bytes 28
  66.9 10.3 %collective-permute-start.2 = (bf16[384,384]{1,0:T(8,128)(2,1)S(1)}, bf16[384,384]{1,0:T(8,128)(2,1)S(1)}, u32[]{:S(2)}, u32[]{:S(2)}) collective-permute-start(bf16[384,384]{1,0:T(8,128)(2,1)S(1)} %get-tuple-element.13), channel_id=1, source_target_pairs={{256,0},{384,128},{0,256},{128,384},{257,1},{385,129},{1,257},{129... | collective-permute-start | bytes 884744 | tf_op jit(solution)/shard_map/ppermute | solution.py:275

commit v5 on v4

--- a/solution.py
+++ b/solution.py
@@ -82,13 +82,13 @@
     copy.wait()
 
     def one_group(group, carry):
-        first = (group // NB * (NY * NB) + group % NB) * MSG2
+        first = (group // NB * (NX // 2 * NY * NB) + group % NB) * MSG2
         for parity in range(2):
             for y in range(NY):
                 lanes = [(2 * y + parity) * K + k for k in range(K)]
                 named = [table[group, lane] for lane in lanes]
                 strips = [table[GROUP // 2 + group, lane] for lane in lanes]
-                base = first + (parity * (NX // 2) * NY + y) * NB * MSG2
+                base = first + (parity * NY + y) * NB * MSG2
                 for l in range(K):
                     for k in range(K):
                         staged[pl.ds(base + (l * K + k) * 2, 2), :] = wide[
@@ -107,7 +107,8 @@
     run = NB * MSG2
     for x in range(NX):
         for y in range(0, NY, 2):
-            chunk = blocks_ref[pl.ds((x * NY + y) * run, 2 * run), :].astype(jnp.float32)
+            place = x % 2 * (NX // 2) + x // 2
+            chunk = blocks_ref[pl.ds((place * NY + y) * run, 2 * run), :].astype(jnp.float32)
             wide[pl.ds((y * NX + x) * run, run), :] = chunk[:run]
             wide[pl.ds(((y + 1) * NX + x) * run, run), :] = chunk[run:]
     left = lax.broadcasted_iota(jnp.int32, (ROWS, V), 1) < HALF
@@ -207,8 +208,7 @@
 
 def shards(amplitudes, factors, tiles, mirror, pair_energy, virt_energy):
     f32, bf16 = jnp.float32, jnp.bfloat16
-    x = lax.axis_index("x")
-    sel = jnp.where(x < NX // 2, 0, 1 - (mirror[0] & 1))
+    sel = jnp.where(lax.axis_index("xa") == 0, 0, 1 - (mirror[0] & 1))
     info = jnp.stack([lax.axis_index(a) for a in ("u", "c")] + [sel, lax.axis_index("y")]).astype(jnp.int32)
     place = jnp.broadcast_to(info.astype(f32)[:, None], (4, V))
     tiles_t = tiles.T
@@ -228,11 +228,11 @@
         compiler_params=pltpu.CompilerParams(vmem_limit_bytes=60 * 1024 * 1024),
         name="spread",
     )(tiles_t, factors)
-    held = lax.all_to_all(spread.reshape(SOURCES, MSG1 // 2, 2, V), ("u", "b", "x"), 0, 0, tiled=True)
+    held = lax.all_to_all(spread.reshape(SOURCES, MSG1 // 2, 2, V), ("u", "b", "xa", "xb"), 0, 0, tiled=True)
     theirs = lax.ppermute(held, "c", [(1, 0), (0, 1)])
     going = lax.dynamic_index_in_dim(amplitudes, 1 - sel, 0, keepdims=False)
-    opposite = [((i + NX // 2) % NX, i) for i in range(NX)]
-    mirror_amps = lax.ppermute(going, "x", opposite)
+    opposite = [(1, 0), (0, 1)]
+    mirror_amps = lax.ppermute(going, "xa", opposite)
 
     held = held.reshape(HELD, V)
     table = pl.pallas_call(
@@ -259,7 +259,7 @@
     )(place, table, held, theirs.reshape(HELD, V))
     selected, mirror_amps = lax.optimization_barrier((selected, mirror_amps))
     blocks = lax.all_to_all(
-        selected.reshape(PLANE, MSG2 // 2, 2, V), ("x", "y", "b"), 0, 0, tiled=True
+        selected.reshape(PLANE, MSG2 // 2, 2, V), ("xb", "xa", "y", "b"), 0, 0, tiled=True
     )
 
     wide_half = jax.ShapeDtypeStruct((WIDTH, NQ * WIDTH), bf16)
@@ -272,7 +272,7 @@
         compiler_params=PARAMS,
         name="ladder",
     )(place, amplitudes, mirror_amps, blocks.reshape(PLANE * MSG2, V))
-    received = lax.ppermute(sent, "x", opposite)
+    received = lax.ppermute(sent, "xa", opposite)
 
     energies = virt_energy.reshape(NT, V)
     outs = (
@@ -309,8 +309,8 @@
 
 
 def solution(mesh):
-    fine = Mesh(mesh.devices.reshape(NX, NU, NB, NC, NY), ("x", "u", "b", "c", "y"))
-    pairs = ("x", "u", "b", "c")
+    fine = Mesh(mesh.devices.reshape(2, NX // 2, NU, NB, NC, NY), ("xa", "xb", "u", "b", "c", "y"))
+    pairs = ("xa", "xb", "u", "b", "c")
     return jax.shard_map(
         shards,
         mesh=fine,

time: 78.7 us -> 78.2 us (level)
  the two profiles are of different devices: /device:TPU:16 before, /device:TPU:2 now
where the time goes in v5:
time: 78.2 us; the launch traced here: 77.8 us
  blocking collectives  31.8 us (41%)
  starting transfers between devices  22.3 us (29%)
  waiting for transfers between devices  13 us (17%)
  Pallas kernels  9.09 us (12%)
  between operations  1.45 us (2%)
    all_to_all x1, blocking collectives, shards(): lax.all_to_all(selected.reshape(PLANE, MSG2 // 2, 2, V), ('xb', 'xa', 'y'...  31.8 us
    all_to_all x1, starting transfers between devices, shards(): lax.all_to_all(spread.reshape(SOURCES, MSG1 // 2, 2, V), ('u', 'b', 'xa',...  13.5 us
    all_to_all x1, waiting for transfers between devices, shards(): lax.all_to_all(spread.reshape(SOURCES, MSG1 // 2, 2, V), ('u', 'b', 'xa',...  6.86 us
    ppermute x1, waiting for transfers between devices, shards(): received = lax.ppermute(sent, 'xa', opposite)  4.9 us
    ppermute x1, starting transfers between devices, shards(): mirror_amps = lax.ppermute(going, 'xa', opposite)  3.98 us
    ppermute x1, starting transfers between devices, shards(): received = lax.ppermute(sent, 'xa', opposite)  2.89 us
    pallas_call x1, Pallas kernels, shards(): pl.pallas_call(own_kernel, out_shape=outs + (jax.ShapeDtypeStruct((WIDTH,...  2.51 us
    pallas_call x1, Pallas kernels, shards(): pl.pallas_call(spread_kernel, out_shape=jax.ShapeDtypeStruct((NU, ROWS *...  1.96 us
  transfers between devices with their start and end apart: 4, of which 3 were waited for; matrix products, arithmetic and copies ran while one was open for 0% of the time, Pallas kernels for 6%

profile of v5, /device:TPU:2, one launch (start us, length us, event | category | flops | bytes accessed | tf_op | source)
XLA Modules:
  0.0 77.8 jit_solution(8510889976831298245)
XLA Ops:
  0.6 0.0 copy-start
  0.6 2.0 %spread.1 = bf16[2,544,128]{2,1,0:T(8,128)(2,1)} custom-call(s32[3,16]{1,0:T(4,128)} %bitcast.21, bf16[2,32,16,64]{3,2,1,0:T(8,128)(2,1)} %factors_hbm.1), custom_call_target="tpu_custom_call" | custom-call | tf_op jit(solution)/shard_map/spread/pallas_call | solution.py:216
  2.6 13.5 %all-to-all-start = ((bf16[32,17,2,128]{3,2,1,0:T(2,128)(2,1)}), bf16[32,17,2,128]{3,2,1,0:T(2,128)(2,1)S(1)}, u32[]{:S(2)}, u32[]{:S(2)}) async-start(bf16[32,17,2,128]{3,2,1,0:T(2,128)(2,1)} %bitcast.23), calls=%async_computation | async-start | bytes 557056 | tf_op jit(solution)/shard_map/all_to_all | solution.py:231
  16.7 0.0 copy-done
  16.8 4.0 %collective-permute-start.1 = (bf16[384,384]{1,0:T(8,128)(2,1)S(1)}, bf16[384,384]{1,0:T(8,128)(2,1)S(1)}, u32[]{:S(2)}, u32[]{:S(2)}) collective-permute-start(bf16[384,384]{1,0:T(8,128)(2,1)S(1)} %dynamic-slice_bitcast_fusion), channel_id=1, source_target_pairs={{256,0},{0,256},{257,1},{1,257},{258,2},{2,258},{259,3},{3,259},{2... | collective-permute-start | bytes 884744 | tf_op jit(solution)/shard_map/ppermute | solution.py:235
  20.8 6.9 %all-to-all-done = bf16[32,17,2,128]{3,2,1,0:T(2,128)(2,1)S(1)} async-done(((bf16[32,17,2,128]{3,2,1,0:T(2,128)(2,1)}), bf16[32,17,2,128]{3,2,1,0:T(2,128)(2,1)S(1)}, u32[]{:S(2)}, u32[]{:S(2)}) %all-to-all-start) | async-done | bytes 278560 | tf_op jit(solution)/shard_map/all_to_all | solution.py:231
  27.7 1.9 %collective-permute-start = (bf16[32,17,2,128]{3,2,1,0:T(2,128)(2,1)S(1)}, bf16[32,17,2,128]{3,2,1,0:T(2,128)(2,1)S(1)}, u32[]{:S(2)}, u32[]{:S(2)}) collective-permute-start(bf16[32,17,2,128]{3,2,1,0:T(2,128)(2,1)S(1)} %all-to-all-done), channel_id=1, source_target_pairs={{8,0},{0,8},{9,1},{1,9},{10,2},{2,10},{11,3},{3,11},{12,4},{4,12},... | collective-permute-start | bytes 835592 | tf_op jit(solution)/shard_map/ppermute | solution.py:232
  29.6 0.1 fusion
  29.7 0.1 broadcast_in_dim.2.place_ref
  29.7 0.1 table.1.table_ref
  29.9 1.2 %collective-permute-done = bf16[32,17,2,128]{3,2,1,0:T(2,128)(2,1)S(1)} collective-permute-done((bf16[32,17,2,128]{3,2,1,0:T(2,128)(2,1)S(1)}, bf16[32,17,2,128]{3,2,1,0:T(2,128)(2,1)S(1)}, u32[]{:S(2)}, u32[]{:S(2)}) %collective-permute-start) | collective-permute-done | bytes 278560 | tf_op jit(solution)/shard_map/ppermute | solution.py:232
  31.1 1.8 %select.1 = bf16[2304,128]{1,0:T(8,128)(2,1)S(1)} custom-call(f32[4,128]{1,0:T(4,128)S(1)} %broadcast_in_dim.2.place_ref, s32[16,128]{1,0:T(8,128)S(1)} %table.1.table_ref, bf16[1088,128]{1,0:T(8,128)(2,1)S(1)} %bitcast.16, bf16[1088,128]{1,0:T(8,128)(2,1)S(1)} %bitcast.19), custom_call_target="tpu_custom_call" | custom-call | tf_op jit(solution)/shard_map/select/pallas_call | solution.py:246
  32.9 0.0 collective-permute-done.1.mirror_amps_ref
  33.0 0.0 copy-start.1
  33.0 0.0 copy-start.2
  33.0 0.0 copy-start.3
  33.0 31.8 %all_to_all.10 = bf16[128,9,2,128]{3,2,1,0:T(2,128)(2,1)S(1)} all-to-all(bf16[128,9,2,128]{3,2,1,0:T(2,128)(2,1)S(1)} %bitcast.17), channel_id=1, replica_groups=mesh['xa'=2,'xb'=2,'u'=2,'b'=4,'c'=2,'y'=8] {'xb','xa','y','b'}, dimensions={0} | all-to-all | bytes 1179648 | tf_op jit(solution)/shard_map/all_to_all | solution.py:261
  64.8 1.6 %ladder.1 = (bf16[384,384]{1,0:T(8,128)(2,1)S(1)}, bf16[384,768]{1,0:T(8,128)(2,1)S(1)}, bf16[384,768]{1,0:T(8,128)(2,1)S(1)}, bf16[384,768]{1,0:T(8,128)(2,1)S(1)}) custom-call(f32[4,128]{1,0:T(4,128)S(1)} %broadcast_in_dim.2.place_ref, bf16[2,384,384]{2,1,0:T(8,128)(2,1)S(1)} %copy-done, bf16[384,384]{1,0:T(8,128)(2,1)S(1)} %collective-permute-done.1.mirror_amps_ref, ...), custom_call_target="tpu_custom_call" | custom-call | tf_op jit(solution)/shard_map/ladder/pallas_call | solution.py:266
  66.4 2.9 %collective-permute-start.2 = (bf16[384,384]{1,0:T(8,128)(2,1)S(1)}, bf16[384,384]{1,0:T(8,128)(2,1)S(1)}, u32[]{:S(2)}, u32[]{:S(2)}) collective-permute-start(bf16[384,384]{1,0:T(8,128)(2,1)S(1)} %get-tuple-element.13), channel_id=1, source_target_pairs={{256,0},{0,256},{257,1},{1,257},{258,2},{2,258},{259,3},{3,259},{2... | collective-permute-start | bytes 884744 | tf_op jit(solution)/shard_map/ppermute | solution.py:275
  69.3 0.0 copy-done.1
  69.3 0.0 copy-done.2
  69.3 0.0 copy-done.3
  69.3 2.5 %own.1 = (f32[2,384,384]{2,1,0:T(8,128)}, bf16[2,384,384]{2,1,0:T(8,128)(2,1)}, f32[384,384]{1,0:T(8,128)S(1)}) custom-call(s32[4]{0:T(128)S(1)} %get-tuple-element.21.info_ref, s32[3,16]{1,0:T(4,128)S(1)} %bitcast.22, f32[2]{0:T(128)S(1)} %copy-done.3, f32[32,128]{1,0:T(8,128)S(1)} %bitcast.20, bf16[2,384,384]{2,1,0:T(8,128)(2,1)S(1)} %copy-done, ...), custom_call_target="tpu_custom_call" | custom-call | flops 452984832 | bytes 1474560 | tf_op jit(solution)/shard_map/own/pallas_call | solution.py:287
  71.8 4.9 %collective-permute-done.2.received_ref = bf16[384,384]{1,0:T(8,128)(2,1)S(1)} collective-permute-done((bf16[384,384]{1,0:T(8,128)(2,1)S(1)}, bf16[384,384]{1,0:T(8,128)(2,1)S(1)}, u32[]{:S(2)}, u32[]{:S(2)}) %collective-permute-start.2) | collective-permute-done | bytes 294944 | tf_op jit(solution)/shard_map/ppermute | solution.py:275
  76.7 1.1 %other.1 = (f32[2,384,384]{2,1,0:T(8,128)}, bf16[2,384,384]{2,1,0:T(8,128)(2,1)}) custom-call(f32[4,128]{1,0:T(4,128)S(1)} %broadcast_in_dim.2.place_ref, bf16[2,384,384]{2,1,0:T(8,128)(2,1)S(1)} %copy-done, bf16[384,384]{1,0:T(8,128)(2,1)S(1)} %collective-permute-done.2.received_ref, ...), custom_call_target="tpu_custom_call", output_to_operand_aliasing={{0}: (4, {}), {1}: (5, {})} | custom-call | flops 589824 | bytes 1474560 | tf_op jit(solution)/shard_map/other/pallas_call | solution.py:297
  (1 shorter events, 0.0 us)
Async XLA Ops:
  0.6 16.1 %copy-start = (bf16[2,384,384]{2,1,0:T(8,128)(2,1)S(1)}, bf16[2,384,384]{2,1,0:T(8,128)(2,1)}, u32[]{:S(2)}) copy-start(bf16[2,384,384]{2,1,0:T(8,128)(2,1)} %amps_ref.5) | copy-start | bytes 1769476
  2.6 25.1 %all-to-all-start = ((bf16[32,17,2,128]{3,2,1,0:T(2,128)(2,1)}), bf16[32,17,2,128]{3,2,1,0:T(2,128)(2,1)S(1)}, u32[]{:S(2)}, u32[]{:S(2)}) async-start(bf16[32,17,2,128]{3,2,1,0:T(2,128)(2,1)} %bitcast.23), calls=%async_computation | async-start | bytes 557056 | tf_op jit(solution)/shard_map/all_to_all | solution.py:231
  16.8 16.1 %collective-permute-start.1 = (bf16[384,384]{1,0:T(8,128)(2,1)S(1)}, bf16[384,384]{1,0:T(8,128)(2,1)S(1)}, u32[]{:S(2)}, u32[]{:S(2)}) collective-permute-start(bf16[384,384]{1,0:T(8,128)(2,1)S(1)} %dynamic-slice_bitcast_fusion), channel_id=1, source_target_pairs={{256,0},{0,256},{257,1},{1,257},{258,2},{2,258},{259,3},{3,259},{2... | collective-permute-start | bytes 884744 | tf_op jit(solution)/shard_map/ppermute | solution.py:235
  27.7 3.4 %collective-permute-start = (bf16[32,17,2,128]{3,2,1,0:T(2,128)(2,1)S(1)}, bf16[32,17,2,128]{3,2,1,0:T(2,128)(2,1)S(1)}, u32[]{:S(2)}, u32[]{:S(2)}) collective-permute-start(bf16[32,17,2,128]{3,2,1,0:T(2,128)(2,1)S(1)} %all-to-all-done), channel_id=1, source_target_pairs={{8,0},{0,8},{9,1},{1,9},{10,2},{2,10},{11,3},{3,11},{12,4},{4,12},... | collective-permute-start | bytes 835592 | tf_op jit(solution)/shard_map/ppermute | solution.py:232
  33.0 36.3 %copy-start.1 = (f32[4096]{0:T(1024)S(1)}, f32[4096]{0:T(1024)}, u32[]{:S(2)}) copy-start(f32[4096]{0:T(1024)} %param.11) | copy-start | bytes 49156
  33.0 36.3 %copy-start.2 = (s32[16,3]{0,1:T(4,128)S(1)}, s32[16,3]{0,1:T(4,128)}, u32[]{:S(2)}) copy-start(s32[16,3]{0,1:T(4,128)} %param.8) | copy-start | bytes 580
  33.0 36.3 %copy-start.3 = (f32[2]{0:T(128)S(1)}, f32[2]{0:T(128)}, u32[]{:S(2)}) copy-start(f32[2]{0:T(128)} %pair_energy_ref.1) | copy-start | bytes 28
  66.4 10.3 %collective-permute-start.2 = (bf16[384,384]{1,0:T(8,128)(2,1)S(1)}, bf16[384,384]{1,0:T(8,128)(2,1)S(1)}, u32[]{:S(2)}, u32[]{:S(2)}) collective-permute-start(bf16[384,384]{1,0:T(8,128)(2,1)S(1)} %get-tuple-element.13), channel_id=1, source_target_pairs={{256,0},{0,256},{257,1},{1,257},{258,2},{2,258},{259,3},{3,259},{2... | collective-permute-start | bytes 884744 | tf_op jit(solution)/shard_map/ppermute | solution.py:275

commit v6 on v5

--- a/solution.py
+++ b/solution.py
@@ -221,7 +221,7 @@
         scratch_shapes=[
             pltpu.SMEM(tiles_t.shape, jnp.int32),
             pltpu.VMEM(factors.shape, bf16),
-            pltpu.VMEM((NQ * NT * ROWS, HALF), f32),
+            pltpu.VMEM(((NQ * NT + 1) * ROWS, HALF), f32),
             pltpu.VMEM((ROWS * MSG1, V), f32),
             pltpu.SemaphoreType.DMA((3,)),
         ],
@@ -249,7 +249,7 @@
         in_specs=[whole()] * 4,
         out_specs=whole(),
         scratch_shapes=[
-            pltpu.VMEM((NC * HELD, V), f32),
+            pltpu.VMEM((NC * HELD + 8, V), f32),
             pltpu.VMEM((PLANE * MSG2, V), f32),
             pltpu.SMEM((GROUP, V), jnp.int32),
             pltpu.SemaphoreType.DMA,
@@ -268,7 +268,7 @@
         out_shape=(jax.ShapeDtypeStruct((WIDTH, WIDTH), bf16), wide_half, wide_half, wide_half),
         in_specs=[whole()] * 4,
         out_specs=(whole(),) * 4,
-        scratch_shapes=[pltpu.VMEM((PLANE * MSG2, V), f32)],
+        scratch_shapes=[pltpu.VMEM((PLANE * MSG2 + 24, V), f32)],
         compiler_params=PARAMS,
         name="ladder",
     )(place, amplitudes, mirror_amps, blocks.reshape(PLANE * MSG2, V))

time: 78.2 us -> 78.2 us (level)
  no operation moved by 1% of the time
where the time goes in v6:
time: 78.2 us; the launch traced here: 77.8 us
  blocking collectives  31.8 us (41%)
  starting transfers between devices  22.3 us (29%)
  waiting for transfers between devices  13 us (17%)
  Pallas kernels  9.09 us (12%)
  between operations  1.45 us (2%)
    all_to_all x1, blocking collectives, shards(): lax.all_to_all(selected.reshape(PLANE, MSG2 // 2, 2, V), ('xb', 'xa', 'y'...  31.8 us
    all_to_all x1, starting transfers between devices, shards(): lax.all_to_all(spread.reshape(SOURCES, MSG1 // 2, 2, V), ('u', 'b', 'xa',...  13.5 us
    all_to_all x1, waiting for transfers between devices, shards(): lax.all_to_all(spread.reshape(SOURCES, MSG1 // 2, 2, V), ('u', 'b', 'xa',...  6.86 us
    ppermute x1, waiting for transfers between devices, shards(): received = lax.ppermute(sent, 'xa', opposite)  4.9 us
    ppermute x1, starting transfers between devices, shards(): mirror_amps = lax.ppermute(going, 'xa', opposite)  3.98 us
    ppermute x1, starting transfers between devices, shards(): received = lax.ppermute(sent, 'xa', opposite)  2.89 us
    pallas_call x1, Pallas kernels, shards(): pl.pallas_call(own_kernel, out_shape=outs + (jax.ShapeDtypeStruct((WIDTH,...  2.51 us
    pallas_call x1, Pallas kernels, shards(): pl.pallas_call(spread_kernel, out_shape=jax.ShapeDtypeStruct((NU, ROWS *...  1.96 us
  transfers between devices with their start and end apart: 4, of which 3 were waited for; matrix products, arithmetic and copies ran while one was open for 0% of the time, Pallas kernels for 6%

profile of v6, /device:TPU:2, one launch (start us, length us, event | category | flops | bytes accessed | tf_op | source)
XLA Modules:
  0.0 77.8 jit_solution(1358063499790663017)
XLA Ops:
  0.6 0.0 copy-start
  0.6 2.0 %spread.1 = bf16[2,544,128]{2,1,0:T(8,128)(2,1)} custom-call(s32[3,16]{1,0:T(4,128)} %bitcast.21, bf16[2,32,16,64]{3,2,1,0:T(8,128)(2,1)} %factors_hbm.1), custom_call_target="tpu_custom_call" | custom-call | tf_op jit(solution)/shard_map/spread/pallas_call | solution.py:216
  2.6 13.5 %all-to-all-start = ((bf16[32,17,2,128]{3,2,1,0:T(2,128)(2,1)}), bf16[32,17,2,128]{3,2,1,0:T(2,128)(2,1)S(1)}, u32[]{:S(2)}, u32[]{:S(2)}) async-start(bf16[32,17,2,128]{3,2,1,0:T(2,128)(2,1)} %bitcast.23), calls=%async_computation | async-start | bytes 557056 | tf_op jit(solution)/shard_map/all_to_all | solution.py:231
  16.7 0.0 copy-done
  16.8 4.0 %collective-permute-start.1 = (bf16[384,384]{1,0:T(8,128)(2,1)S(1)}, bf16[384,384]{1,0:T(8,128)(2,1)S(1)}, u32[]{:S(2)}, u32[]{:S(2)}) collective-permute-start(bf16[384,384]{1,0:T(8,128)(2,1)S(1)} %dynamic-slice_bitcast_fusion), channel_id=1, source_target_pairs={{256,0},{0,256},{257,1},{1,257},{258,2},{2,258},{259,3},{3,259},{2... | collective-permute-start | bytes 884744 | tf_op jit(solution)/shard_map/ppermute | solution.py:235
  20.8 6.9 %all-to-all-done = bf16[32,17,2,128]{3,2,1,0:T(2,128)(2,1)S(1)} async-done(((bf16[32,17,2,128]{3,2,1,0:T(2,128)(2,1)}), bf16[32,17,2,128]{3,2,1,0:T(2,128)(2,1)S(1)}, u32[]{:S(2)}, u32[]{:S(2)}) %all-to-all-start) | async-done | bytes 278560 | tf_op jit(solution)/shard_map/all_to_all | solution.py:231
  27.7 1.9 %collective-permute-start = (bf16[32,17,2,128]{3,2,1,0:T(2,128)(2,1)S(1)}, bf16[32,17,2,128]{3,2,1,0:T(2,128)(2,1)S(1)}, u32[]{:S(2)}, u32[]{:S(2)}) collective-permute-start(bf16[32,17,2,128]{3,2,1,0:T(2,128)(2,1)S(1)} %all-to-all-done), channel_id=1, source_target_pairs={{8,0},{0,8},{9,1},{1,9},{10,2},{2,10},{11,3},{3,11},{12,4},{4,12},... | collective-permute-start | bytes 835592 | tf_op jit(solution)/shard_map/ppermute | solution.py:232
  29.6 0.1 fusion
  29.7 0.1 broadcast_in_dim.2.place_ref
  29.7 0.1 table.1.table_ref
  29.9 1.2 %collective-permute-done = bf16[32,17,2,128]{3,2,1,0:T(2,128)(2,1)S(1)} collective-permute-done((bf16[32,17,2,128]{3,2,1,0:T(2,128)(2,1)S(1)}, bf16[32,17,2,128]{3,2,1,0:T(2,128)(2,1)S(1)}, u32[]{:S(2)}, u32[]{:S(2)}) %collective-permute-start) | collective-permute-done | bytes 278560 | tf_op jit(solution)/shard_map/ppermute | solution.py:232
  31.1 1.8 %select.1 = bf16[2304,128]{1,0:T(8,128)(2,1)S(1)} custom-call(f32[4,128]{1,0:T(4,128)S(1)} %broadcast_in_dim.2.place_ref, s32[16,128]{1,0:T(8,128)S(1)} %table.1.table_ref, bf16[1088,128]{1,0:T(8,128)(2,1)S(1)} %bitcast.16, bf16[1088,128]{1,0:T(8,128)(2,1)S(1)} %bitcast.19), custom_call_target="tpu_custom_call" | custom-call | tf_op jit(solution)/shard_map/select/pallas_call | solution.py:246
  32.9 0.0 collective-permute-done.1.mirror_amps_ref
  33.0 0.0 copy-start.1
  33.0 0.0 copy-start.2
  33.0 0.0 copy-start.3
  33.0 31.8 %all_to_all.10 = bf16[128,9,2,128]{3,2,1,0:T(2,128)(2,1)S(1)} all-to-all(bf16[128,9,2,128]{3,2,1,0:T(2,128)(2,1)S(1)} %bitcast.17), channel_id=1, replica_groups=mesh['xa'=2,'xb'=2,'u'=2,'b'=4,'c'=2,'y'=8] {'xb','xa','y','b'}, dimensions={0} | all-to-all | bytes 1179648 | tf_op jit(solution)/shard_map/all_to_all | solution.py:261
  64.8 1.6 %ladder.1 = (bf16[384,384]{1,0:T(8,128)(2,1)S(1)}, bf16[384,768]{1,0:T(8,128)(2,1)S(1)}, bf16[384,768]{1,0:T(8,128)(2,1)S(1)}, bf16[384,768]{1,0:T(8,128)(2,1)S(1)}) custom-call(f32[4,128]{1,0:T(4,128)S(1)} %broadcast_in_dim.2.place_ref, bf16[2,384,384]{2,1,0:T(8,128)(2,1)S(1)} %copy-done, bf16[384,384]{1,0:T(8,128)(2,1)S(1)} %collective-permute-done.1.mirror_amps_ref, ...), custom_call_target="tpu_custom_call" | custom-call | tf_op jit(solution)/shard_map/ladder/pallas_call | solution.py:266
  66.4 2.9 %collective-permute-start.2 = (bf16[384,384]{1,0:T(8,128)(2,1)S(1)}, bf16[384,384]{1,0:T(8,128)(2,1)S(1)}, u32[]{:S(2)}, u32[]{:S(2)}) collective-permute-start(bf16[384,384]{1,0:T(8,128)(2,1)S(1)} %get-tuple-element.13), channel_id=1, source_target_pairs={{256,0},{0,256},{257,1},{1,257},{258,2},{2,258},{259,3},{3,259},{2... | collective-permute-start | bytes 884744 | tf_op jit(solution)/shard_map/ppermute | solution.py:275
  69.3 0.0 copy-done.1
  69.3 0.0 copy-done.2
  69.3 0.0 copy-done.3
  69.3 2.5 %own.1 = (f32[2,384,384]{2,1,0:T(8,128)}, bf16[2,384,384]{2,1,0:T(8,128)(2,1)}, f32[384,384]{1,0:T(8,128)S(1)}) custom-call(s32[4]{0:T(128)S(1)} %get-tuple-element.21.info_ref, s32[3,16]{1,0:T(4,128)S(1)} %bitcast.22, f32[2]{0:T(128)S(1)} %copy-done.3, f32[32,128]{1,0:T(8,128)S(1)} %bitcast.20, bf16[2,384,384]{2,1,0:T(8,128)(2,1)S(1)} %copy-done, ...), custom_call_target="tpu_custom_call" | custom-call | flops 452984832 | bytes 1474560 | tf_op jit(solution)/shard_map/own/pallas_call | solution.py:287
  71.8 4.9 %collective-permute-done.2.received_ref = bf16[384,384]{1,0:T(8,128)(2,1)S(1)} collective-permute-done((bf16[384,384]{1,0:T(8,128)(2,1)S(1)}, bf16[384,384]{1,0:T(8,128)(2,1)S(1)}, u32[]{:S(2)}, u32[]{:S(2)}) %collective-permute-start.2) | collective-permute-done | bytes 294944 | tf_op jit(solution)/shard_map/ppermute | solution.py:275
  76.7 1.1 %other.1 = (f32[2,384,384]{2,1,0:T(8,128)}, bf16[2,384,384]{2,1,0:T(8,128)(2,1)}) custom-call(f32[4,128]{1,0:T(4,128)S(1)} %broadcast_in_dim.2.place_ref, bf16[2,384,384]{2,1,0:T(8,128)(2,1)S(1)} %copy-done, bf16[384,384]{1,0:T(8,128)(2,1)S(1)} %collective-permute-done.2.received_ref, ...), custom_call_target="tpu_custom_call", output_to_operand_aliasing={{0}: (4, {}), {1}: (5, {})} | custom-call | flops 589824 | bytes 1474560 | tf_op jit(solution)/shard_map/other/pallas_call | solution.py:297
  (1 shorter events, 0.0 us)
Async XLA Ops:
  0.6 16.1 %copy-start = (bf16[2,384,384]{2,1,0:T(8,128)(2,1)S(1)}, bf16[2,384,384]{2,1,0:T(8,128)(2,1)}, u32[]{:S(2)}) copy-start(bf16[2,384,384]{2,1,0:T(8,128)(2,1)} %amps_ref.5) | copy-start | bytes 1769476
  2.6 25.1 %all-to-all-start = ((bf16[32,17,2,128]{3,2,1,0:T(2,128)(2,1)}), bf16[32,17,2,128]{3,2,1,0:T(2,128)(2,1)S(1)}, u32[]{:S(2)}, u32[]{:S(2)}) async-start(bf16[32,17,2,128]{3,2,1,0:T(2,128)(2,1)} %bitcast.23), calls=%async_computation | async-start | bytes 557056 | tf_op jit(solution)/shard_map/all_to_all | solution.py:231
  16.8 16.1 %collective-permute-start.1 = (bf16[384,384]{1,0:T(8,128)(2,1)S(1)}, bf16[384,384]{1,0:T(8,128)(2,1)S(1)}, u32[]{:S(2)}, u32[]{:S(2)}) collective-permute-start(bf16[384,384]{1,0:T(8,128)(2,1)S(1)} %dynamic-slice_bitcast_fusion), channel_id=1, source_target_pairs={{256,0},{0,256},{257,1},{1,257},{258,2},{2,258},{259,3},{3,259},{2... | collective-permute-start | bytes 884744 | tf_op jit(solution)/shard_map/ppermute | solution.py:235
  27.7 3.4 %collective-permute-start = (bf16[32,17,2,128]{3,2,1,0:T(2,128)(2,1)S(1)}, bf16[32,17,2,128]{3,2,1,0:T(2,128)(2,1)S(1)}, u32[]{:S(2)}, u32[]{:S(2)}) collective-permute-start(bf16[32,17,2,128]{3,2,1,0:T(2,128)(2,1)S(1)} %all-to-all-done), channel_id=1, source_target_pairs={{8,0},{0,8},{9,1},{1,9},{10,2},{2,10},{11,3},{3,11},{12,4},{4,12},... | collective-permute-start | bytes 835592 | tf_op jit(solution)/shard_map/ppermute | solution.py:232
  33.0 36.3 %copy-start.1 = (f32[4096]{0:T(1024)S(1)}, f32[4096]{0:T(1024)}, u32[]{:S(2)}) copy-start(f32[4096]{0:T(1024)} %param.11) | copy-start | bytes 49156
  33.0 36.3 %copy-start.2 = (s32[16,3]{0,1:T(4,128)S(1)}, s32[16,3]{0,1:T(4,128)}, u32[]{:S(2)}) copy-start(s32[16,3]{0,1:T(4,128)} %param.8) | copy-start | bytes 580
  33.0 36.3 %copy-start.3 = (f32[2]{0:T(128)S(1)}, f32[2]{0:T(128)}, u32[]{:S(2)}) copy-start(f32[2]{0:T(128)} %pair_energy_ref.1) | copy-start | bytes 28
  66.4 10.3 %collective-permute-start.2 = (bf16[384,384]{1,0:T(8,128)(2,1)S(1)}, bf16[384,384]{1,0:T(8,128)(2,1)S(1)}, u32[]{:S(2)}, u32[]{:S(2)}) collective-permute-start(bf16[384,384]{1,0:T(8,128)(2,1)S(1)} %get-tuple-element.13), channel_id=1, source_target_pairs={{256,0},{0,256},{257,1},{1,257},{258,2},{2,258},{259,3},{3,259},{2... | collective-permute-start | bytes 884744 | tf_op jit(solution)/shard_map/ppermute | solution.py:275

commit v7 on v6

--- a/solution.py
+++ b/solution.py
@@ -63,14 +63,17 @@
 
 
 def table_kernel(place_ref, held_ref, out_ref):
+    which = lax.rem(lax.broadcasted_iota(jnp.int32, (1, V), 1), K)
     start = pl.multiple_of(scalar_of(place_ref[0:1]) * (ROWS * MSG1), 16)
     for group in range(GROUP // 2):
         row = (group % NB * NX + group // NB) * MSG1 + NT
         block = held_ref[pl.ds(pl.multiple_of(start + row // 16 * 16, 16), 16), :].astype(jnp.float32)
         named = block[row % 16 : row % 16 + 1].astype(jnp.int32)
         strip = ((named >> 2) & 1) * ROWS + (named & (NB - 1)) * NX + (named >> 3)
-        out_ref[pl.ds(group, 1), :] = 2 * named
-        out_ref[pl.ds(GROUP // 2 + group, 1), :] = 2 * MSG1 * strip
+        for k in range(K):
+            turned = [named if l == k else pltpu.roll(named, (l - k) % V, 1) for l in range(K)]
+            row_tile = jnp.where(which == 0, turned[0], jnp.where(which == 1, turned[1], turned[2]))
+            out_ref[pl.ds(group * K + k, 1), :] = 2 * MSG1 * strip + 2 * row_tile
 
 
 def select_kernel(place_ref, table_ref, mine_ref, theirs_ref, out_ref, wide, staged, table, sem):
@@ -85,14 +88,12 @@
         first = (group // NB * (NX // 2 * NY * NB) + group % NB) * MSG2
         for parity in range(2):
             for y in range(NY):
-                lanes = [(2 * y + parity) * K + k for k in range(K)]
-                named = [table[group, lane] for lane in lanes]
-                strips = [table[GROUP // 2 + group, lane] for lane in lanes]
+                member = 2 * y + parity
                 base = first + (parity * NY + y) * NB * MSG2
                 for l in range(K):
                     for k in range(K):
                         staged[pl.ds(base + (l * K + k) * 2, 2), :] = wide[
-                            pl.ds(pl.multiple_of(strips[l] + named[k], 2), 2), :
+                            pl.ds(pl.multiple_of(table[group * K + k, member * K + l], 2), 2), :
                         ]
         return carry
 
@@ -237,7 +238,7 @@
     held = held.reshape(HELD, V)
     table = pl.pallas_call(
         table_kernel,
-        out_shape=jax.ShapeDtypeStruct((GROUP, V), jnp.int32),
+        out_shape=jax.ShapeDtypeStruct((GROUP // 2 * K, V), jnp.int32),
         in_specs=[whole(), whole()],
         out_specs=whole(),
         compiler_params=PARAMS,
@@ -251,7 +252,7 @@
         scratch_shapes=[
             pltpu.VMEM((NC * HELD + 8, V), f32),
             pltpu.VMEM((PLANE * MSG2, V), f32),
-            pltpu.SMEM((GROUP, V), jnp.int32),
+            pltpu.SMEM((GROUP // 2 * K, V), jnp.int32),
             pltpu.SemaphoreType.DMA,
         ],
         compiler_params=PARAMS,

time: 78.2 us -> 78.1 us (level)
  no operation moved by 1% of the time
where the time goes in v7:
time: 78.1 us; the launch traced here: 77.8 us
  blocking collectives  31.8 us (41%)
  starting transfers between devices  22.3 us (29%)
  waiting for transfers between devices  12.9 us (17%)
  Pallas kernels  9.13 us (12%)
  between operations  1.44 us (2%)
    all_to_all x1, blocking collectives, shards(): lax.all_to_all(selected.reshape(PLANE, MSG2 // 2, 2, V), ('xb', 'xa', 'y'...  31.8 us
    all_to_all x1, starting transfers between devices, shards(): lax.all_to_all(spread.reshape(SOURCES, MSG1 // 2, 2, V), ('u', 'b', 'xa',...  13.5 us
    all_to_all x1, waiting for transfers between devices, shards(): lax.all_to_all(spread.reshape(SOURCES, MSG1 // 2, 2, V), ('u', 'b', 'xa',...  6.86 us
    ppermute x1, waiting for transfers between devices, shards(): received = lax.ppermute(sent, 'xa', opposite)  4.9 us
    ppermute x1, starting transfers between devices, shards(): mirror_amps = lax.ppermute(going, 'xa', opposite)  3.98 us
    ppermute x1, starting transfers between devices, shards(): received = lax.ppermute(sent, 'xa', opposite)  2.9 us
    pallas_call x1, Pallas kernels, shards(): pl.pallas_call(own_kernel, out_shape=outs + (jax.ShapeDtypeStruct((WIDTH,...  2.51 us
    pallas_call x1, Pallas kernels, shards(): pl.pallas_call(spread_kernel, out_shape=jax.ShapeDtypeStruct((NU, ROWS *...  1.96 us
  transfers between devices with their start and end apart: 4, of which 3 were waited for; matrix products, arithmetic and copies ran while one was open for 0% of the time, Pallas kernels for 6%

profile of v7, /device:TPU:2, one launch (start us, length us, event | category | flops | bytes accessed | tf_op | source)
XLA Modules:
  0.0 77.8 jit_solution(9616851070838101317)
XLA Ops:
  0.6 0.0 copy-start
  0.6 2.0 %spread.1 = bf16[2,544,128]{2,1,0:T(8,128)(2,1)} custom-call(s32[3,16]{1,0:T(4,128)} %bitcast.21, bf16[2,32,16,64]{3,2,1,0:T(8,128)(2,1)} %factors_hbm.1), custom_call_target="tpu_custom_call" | custom-call | tf_op jit(solution)/shard_map/spread/pallas_call | solution.py:217
  2.6 13.5 %all-to-all-start = ((bf16[32,17,2,128]{3,2,1,0:T(2,128)(2,1)}), bf16[32,17,2,128]{3,2,1,0:T(2,128)(2,1)S(1)}, u32[]{:S(2)}, u32[]{:S(2)}) async-start(bf16[32,17,2,128]{3,2,1,0:T(2,128)(2,1)} %bitcast.23), calls=%async_computation | async-start | bytes 557056 | tf_op jit(solution)/shard_map/all_to_all | solution.py:232
  16.7 0.0 copy-done
  16.8 4.0 %collective-permute-start.1 = (bf16[384,384]{1,0:T(8,128)(2,1)S(1)}, bf16[384,384]{1,0:T(8,128)(2,1)S(1)}, u32[]{:S(2)}, u32[]{:S(2)}) collective-permute-start(bf16[384,384]{1,0:T(8,128)(2,1)S(1)} %dynamic-slice_bitcast_fusion), channel_id=1, source_target_pairs={{256,0},{0,256},{257,1},{1,257},{258,2},{2,258},{259,3},{3,259},{2... | collective-permute-start | bytes 884744 | tf_op jit(solution)/shard_map/ppermute | solution.py:236
  20.8 6.9 %all-to-all-done = bf16[32,17,2,128]{3,2,1,0:T(2,128)(2,1)S(1)} async-done(((bf16[32,17,2,128]{3,2,1,0:T(2,128)(2,1)}), bf16[32,17,2,128]{3,2,1,0:T(2,128)(2,1)S(1)}, u32[]{:S(2)}, u32[]{:S(2)}) %all-to-all-start) | async-done | bytes 278560 | tf_op jit(solution)/shard_map/all_to_all | solution.py:232
  27.7 1.9 %collective-permute-start = (bf16[32,17,2,128]{3,2,1,0:T(2,128)(2,1)S(1)}, bf16[32,17,2,128]{3,2,1,0:T(2,128)(2,1)S(1)}, u32[]{:S(2)}, u32[]{:S(2)}) collective-permute-start(bf16[32,17,2,128]{3,2,1,0:T(2,128)(2,1)S(1)} %all-to-all-done), channel_id=1, source_target_pairs={{8,0},{0,8},{9,1},{1,9},{10,2},{2,10},{11,3},{3,11},{12,4},{4,12},... | collective-permute-start | bytes 835592 | tf_op jit(solution)/shard_map/ppermute | solution.py:233
  29.6 0.1 fusion
  29.7 0.1 broadcast_in_dim.2.place_ref
  29.7 0.2 table.1.table_ref
  30.0 1.1 %collective-permute-done = bf16[32,17,2,128]{3,2,1,0:T(2,128)(2,1)S(1)} collective-permute-done((bf16[32,17,2,128]{3,2,1,0:T(2,128)(2,1)S(1)}, bf16[32,17,2,128]{3,2,1,0:T(2,128)(2,1)S(1)}, u32[]{:S(2)}, u32[]{:S(2)}) %collective-permute-start) | collective-permute-done | bytes 278560 | tf_op jit(solution)/shard_map/ppermute | solution.py:233
  31.1 1.8 %select.1 = bf16[2304,128]{1,0:T(8,128)(2,1)S(1)} custom-call(f32[4,128]{1,0:T(4,128)S(1)} %broadcast_in_dim.2.place_ref, s32[24,128]{1,0:T(8,128)S(1)} %table.1.table_ref, bf16[1088,128]{1,0:T(8,128)(2,1)S(1)} %bitcast.16, bf16[1088,128]{1,0:T(8,128)(2,1)S(1)} %bitcast.19), custom_call_target="tpu_custom_call" | custom-call | tf_op jit(solution)/shard_map/select/pallas_call | solution.py:247
  32.9 0.0 collective-permute-done.1.mirror_amps_ref
  32.9 0.0 copy-start.1
  32.9 0.0 copy-start.2
  32.9 0.0 copy-start.3
  32.9 31.8 %all_to_all.10 = bf16[128,9,2,128]{3,2,1,0:T(2,128)(2,1)S(1)} all-to-all(bf16[128,9,2,128]{3,2,1,0:T(2,128)(2,1)S(1)} %bitcast.17), channel_id=1, replica_groups=mesh['xa'=2,'xb'=2,'u'=2,'b'=4,'c'=2,'y'=8] {'xb','xa','y','b'}, dimensions={0} | all-to-all | bytes 1179648 | tf_op jit(solution)/shard_map/all_to_all | solution.py:262
  64.8 1.6 %ladder.1 = (bf16[384,384]{1,0:T(8,128)(2,1)S(1)}, bf16[384,768]{1,0:T(8,128)(2,1)S(1)}, bf16[384,768]{1,0:T(8,128)(2,1)S(1)}, bf16[384,768]{1,0:T(8,128)(2,1)S(1)}) custom-call(f32[4,128]{1,0:T(4,128)S(1)} %broadcast_in_dim.2.place_ref, bf16[2,384,384]{2,1,0:T(8,128)(2,1)S(1)} %copy-done, bf16[384,384]{1,0:T(8,128)(2,1)S(1)} %collective-permute-done.1.mirror_amps_ref, ...), custom_call_target="tpu_custom_call" | custom-call | tf_op jit(solution)/shard_map/ladder/pallas_call | solution.py:267
  66.3 2.9 %collective-permute-start.2 = (bf16[384,384]{1,0:T(8,128)(2,1)S(1)}, bf16[384,384]{1,0:T(8,128)(2,1)S(1)}, u32[]{:S(2)}, u32[]{:S(2)}) collective-permute-start(bf16[384,384]{1,0:T(8,128)(2,1)S(1)} %get-tuple-element.13), channel_id=1, source_target_pairs={{256,0},{0,256},{257,1},{1,257},{258,2},{2,258},{259,3},{3,259},{2... | collective-permute-start | bytes 884744 | tf_op jit(solution)/shard_map/ppermute | solution.py:276
  69.2 0.0 copy-done.1
  69.2 0.0 copy-done.2
  69.3 0.0 copy-done.3
  69.3 2.5 %own.1 = (f32[2,384,384]{2,1,0:T(8,128)}, bf16[2,384,384]{2,1,0:T(8,128)(2,1)}, f32[384,384]{1,0:T(8,128)S(1)}) custom-call(s32[4]{0:T(128)S(1)} %get-tuple-element.21.info_ref, s32[3,16]{1,0:T(4,128)S(1)} %bitcast.22, f32[2]{0:T(128)S(1)} %copy-done.3, f32[32,128]{1,0:T(8,128)S(1)} %bitcast.20, bf16[2,384,384]{2,1,0:T(8,128)(2,1)S(1)} %copy-done, ...), custom_call_target="tpu_custom_call" | custom-call | flops 452984832 | bytes 1474560 | tf_op jit(solution)/shard_map/own/pallas_call | solution.py:288
  71.8 4.9 %collective-permute-done.2.received_ref = bf16[384,384]{1,0:T(8,128)(2,1)S(1)} collective-permute-done((bf16[384,384]{1,0:T(8,128)(2,1)S(1)}, bf16[384,384]{1,0:T(8,128)(2,1)S(1)}, u32[]{:S(2)}, u32[]{:S(2)}) %collective-permute-start.2) | collective-permute-done | bytes 294944 | tf_op jit(solution)/shard_map/ppermute | solution.py:276
  76.7 1.1 %other.1 = (f32[2,384,384]{2,1,0:T(8,128)}, bf16[2,384,384]{2,1,0:T(8,128)(2,1)}) custom-call(f32[4,128]{1,0:T(4,128)S(1)} %broadcast_in_dim.2.place_ref, bf16[2,384,384]{2,1,0:T(8,128)(2,1)S(1)} %copy-done, bf16[384,384]{1,0:T(8,128)(2,1)S(1)} %collective-permute-done.2.received_ref, ...), custom_call_target="tpu_custom_call", output_to_operand_aliasing={{0}: (4, {}), {1}: (5, {})} | custom-call | flops 589824 | bytes 1474560 | tf_op jit(solution)/shard_map/other/pallas_call | solution.py:298
  (1 shorter events, 0.0 us)
Async XLA Ops:
  0.6 16.1 %copy-start = (bf16[2,384,384]{2,1,0:T(8,128)(2,1)S(1)}, bf16[2,384,384]{2,1,0:T(8,128)(2,1)}, u32[]{:S(2)}) copy-start(bf16[2,384,384]{2,1,0:T(8,128)(2,1)} %amps_ref.5) | copy-start | bytes 1769476
  2.6 25.1 %all-to-all-start = ((bf16[32,17,2,128]{3,2,1,0:T(2,128)(2,1)}), bf16[32,17,2,128]{3,2,1,0:T(2,128)(2,1)S(1)}, u32[]{:S(2)}, u32[]{:S(2)}) async-start(bf16[32,17,2,128]{3,2,1,0:T(2,128)(2,1)} %bitcast.23), calls=%async_computation | async-start | bytes 557056 | tf_op jit(solution)/shard_map/all_to_all | solution.py:232
  16.8 16.1 %collective-permute-start.1 = (bf16[384,384]{1,0:T(8,128)(2,1)S(1)}, bf16[384,384]{1,0:T(8,128)(2,1)S(1)}, u32[]{:S(2)}, u32[]{:S(2)}) collective-permute-start(bf16[384,384]{1,0:T(8,128)(2,1)S(1)} %dynamic-slice_bitcast_fusion), channel_id=1, source_target_pairs={{256,0},{0,256},{257,1},{1,257},{258,2},{2,258},{259,3},{3,259},{2... | collective-permute-start | bytes 884744 | tf_op jit(solution)/shard_map/ppermute | solution.py:236
  27.7 3.4 %collective-permute-start = (bf16[32,17,2,128]{3,2,1,0:T(2,128)(2,1)S(1)}, bf16[32,17,2,128]{3,2,1,0:T(2,128)(2,1)S(1)}, u32[]{:S(2)}, u32[]{:S(2)}) collective-permute-start(bf16[32,17,2,128]{3,2,1,0:T(2,128)(2,1)S(1)} %all-to-all-done), channel_id=1, source_target_pairs={{8,0},{0,8},{9,1},{1,9},{10,2},{2,10},{11,3},{3,11},{12,4},{4,12},... | collective-permute-start | bytes 835592 | tf_op jit(solution)/shard_map/ppermute | solution.py:233
  32.9 36.3 %copy-start.1 = (f32[4096]{0:T(1024)S(1)}, f32[4096]{0:T(1024)}, u32[]{:S(2)}) copy-start(f32[4096]{0:T(1024)} %param.11) | copy-start | bytes 49156
  32.9 36.3 %copy-start.2 = (s32[16,3]{0,1:T(4,128)S(1)}, s32[16,3]{0,1:T(4,128)}, u32[]{:S(2)}) copy-start(s32[16,3]{0,1:T(4,128)} %param.8) | copy-start | bytes 580
  32.9 36.3 %copy-start.3 = (f32[2]{0:T(128)S(1)}, f32[2]{0:T(128)}, u32[]{:S(2)}) copy-start(f32[2]{0:T(128)} %pair_energy_ref.1) | copy-start | bytes 28
  66.3 10.4 %collective-permute-start.2 = (bf16[384,384]{1,0:T(8,128)(2,1)S(1)}, bf16[384,384]{1,0:T(8,128)(2,1)S(1)}, u32[]{:S(2)}, u32[]{:S(2)}) collective-permute-start(bf16[384,384]{1,0:T(8,128)(2,1)S(1)} %get-tuple-element.13), channel_id=1, source_target_pairs={{256,0},{0,256},{257,1},{1,257},{258,2},{2,258},{259,3},{3,259},{2... | collective-permute-start | bytes 884744 | tf_op jit(solution)/shard_map/ppermute | solution.py:276

commit v8 on v7

--- a/solution.py
+++ b/solution.py
@@ -152,20 +152,19 @@
 
 def write_pair(slot, denominator_of, residual_of, amps_ref, residual_out, updated_out, residual_buf, updated_buf, sems):
     copies = []
-    for step in range(K):
-        band = pl.ds(step * V, V)
-        residual = residual_of(band)
-        residual_buf[band, :] = residual
-        updated_buf[band, :] = (
-            amps_ref[slot, band, :].astype(jnp.float32) - residual / denominator_of(step)
-        ).astype(jnp.bfloat16)
-        for buf, out, sem in (
-            (residual_buf, residual_out, sems.at[0, step]),
-            (updated_buf, updated_out, sems.at[1, step]),
-        ):
-            copy = pltpu.make_async_copy(buf.at[band, :], out.at[slot, band, :], sem)
-            copy.start()
-            copies.append(copy)
+
+    def send(buf, out, band, sem):
+        copies.append(pltpu.make_async_copy(buf.at[band, :], out.at[slot, band, :], sem))
+        copies[-1].start()
+
+    bands = [pl.ds(step * V, V) for step in range(K)]
+    for step, band in enumerate(bands):
+        residual_buf[band, :] = residual_of(band)
+        send(residual_buf, residual_out, band, sems.at[0, step])
+    for step, band in enumerate(bands):
+        change = residual_buf[band, :] / denominator_of(step)
+        updated_buf[band, :] = (amps_ref[slot, band, :].astype(jnp.float32) - change).astype(jnp.bfloat16)
+        send(updated_buf, updated_out, band, sems.at[1, step])
     for copy in copies:
         copy.wait()
 

time: 78.1 us -> 78.1 us (level)
  no operation moved by 1% of the time
where the time goes in v8:
time: 78.1 us; the launch traced here: 77.8 us
  blocking collectives  31.8 us (41%)
  starting transfers between devices  22.3 us (29%)
  waiting for transfers between devices  12.8 us (16%)
  Pallas kernels  9.19 us (12%)
  between operations  1.44 us (2%)
    all_to_all x1, blocking collectives, shards(): lax.all_to_all(selected.reshape(PLANE, MSG2 // 2, 2, V), ('xb', 'xa', 'y'...  31.8 us
    all_to_all x1, starting transfers between devices, shards(): lax.all_to_all(spread.reshape(SOURCES, MSG1 // 2, 2, V), ('u', 'b', 'xa',...  13.5 us
    all_to_all x1, waiting for transfers between devices, shards(): lax.all_to_all(spread.reshape(SOURCES, MSG1 // 2, 2, V), ('u', 'b', 'xa',...  6.86 us
    ppermute x1, waiting for transfers between devices, shards(): received = lax.ppermute(sent, 'xa', opposite)  4.84 us
    ppermute x1, starting transfers between devices, shards(): mirror_amps = lax.ppermute(going, 'xa', opposite)  3.98 us
    ppermute x1, starting transfers between devices, shards(): received = lax.ppermute(sent, 'xa', opposite)  2.9 us
    pallas_call x1, Pallas kernels, shards(): pl.pallas_call(own_kernel, out_shape=outs + (jax.ShapeDtypeStruct((WIDTH,...  2.57 us
    pallas_call x1, Pallas kernels, shards(): pl.pallas_call(spread_kernel, out_shape=jax.ShapeDtypeStruct((NU, ROWS *...  1.96 us
  transfers between devices with their start and end apart: 4, of which 3 were waited for; matrix products, arithmetic and copies ran while one was open for 0% of the time, Pallas kernels for 6%

profile of v8, /device:TPU:2, one launch (start us, length us, event | category | flops | bytes accessed | tf_op | source)
XLA Modules:
  0.0 77.8 jit_solution(17597881676685534787)
XLA Ops:
  0.6 0.0 copy-start
  0.6 2.0 %spread.1 = bf16[2,544,128]{2,1,0:T(8,128)(2,1)} custom-call(s32[3,16]{1,0:T(4,128)} %bitcast.21, bf16[2,32,16,64]{3,2,1,0:T(8,128)(2,1)} %factors_hbm.1), custom_call_target="tpu_custom_call" | custom-call | tf_op jit(solution)/shard_map/spread/pallas_call | solution.py:216
  2.6 13.5 %all-to-all-start = ((bf16[32,17,2,128]{3,2,1,0:T(2,128)(2,1)}), bf16[32,17,2,128]{3,2,1,0:T(2,128)(2,1)S(1)}, u32[]{:S(2)}, u32[]{:S(2)}) async-start(bf16[32,17,2,128]{3,2,1,0:T(2,128)(2,1)} %bitcast.23), calls=%async_computation | async-start | bytes 557056 | tf_op jit(solution)/shard_map/all_to_all | solution.py:231
  16.7 0.0 copy-done
  16.8 4.0 %collective-permute-start.1 = (bf16[384,384]{1,0:T(8,128)(2,1)S(1)}, bf16[384,384]{1,0:T(8,128)(2,1)S(1)}, u32[]{:S(2)}, u32[]{:S(2)}) collective-permute-start(bf16[384,384]{1,0:T(8,128)(2,1)S(1)} %dynamic-slice_bitcast_fusion), channel_id=1, source_target_pairs={{256,0},{0,256},{257,1},{1,257},{258,2},{2,258},{259,3},{3,259},{2... | collective-permute-start | bytes 884744 | tf_op jit(solution)/shard_map/ppermute | solution.py:235
  20.8 6.9 %all-to-all-done = bf16[32,17,2,128]{3,2,1,0:T(2,128)(2,1)S(1)} async-done(((bf16[32,17,2,128]{3,2,1,0:T(2,128)(2,1)}), bf16[32,17,2,128]{3,2,1,0:T(2,128)(2,1)S(1)}, u32[]{:S(2)}, u32[]{:S(2)}) %all-to-all-start) | async-done | bytes 278560 | tf_op jit(solution)/shard_map/all_to_all | solution.py:231
  27.7 1.9 %collective-permute-start = (bf16[32,17,2,128]{3,2,1,0:T(2,128)(2,1)S(1)}, bf16[32,17,2,128]{3,2,1,0:T(2,128)(2,1)S(1)}, u32[]{:S(2)}, u32[]{:S(2)}) collective-permute-start(bf16[32,17,2,128]{3,2,1,0:T(2,128)(2,1)S(1)} %all-to-all-done), channel_id=1, source_target_pairs={{8,0},{0,8},{9,1},{1,9},{10,2},{2,10},{11,3},{3,11},{12,4},{4,12},... | collective-permute-start | bytes 835592 | tf_op jit(solution)/shard_map/ppermute | solution.py:232
  29.6 0.1 fusion
  29.7 0.1 broadcast_in_dim.2.place_ref
  29.7 0.2 table.1.table_ref
  30.0 1.1 %collective-permute-done = bf16[32,17,2,128]{3,2,1,0:T(2,128)(2,1)S(1)} collective-permute-done((bf16[32,17,2,128]{3,2,1,0:T(2,128)(2,1)S(1)}, bf16[32,17,2,128]{3,2,1,0:T(2,128)(2,1)S(1)}, u32[]{:S(2)}, u32[]{:S(2)}) %collective-permute-start) | collective-permute-done | bytes 278560 | tf_op jit(solution)/shard_map/ppermute | solution.py:232
  31.1 1.8 %select.1 = bf16[2304,128]{1,0:T(8,128)(2,1)S(1)} custom-call(f32[4,128]{1,0:T(4,128)S(1)} %broadcast_in_dim.2.place_ref, s32[24,128]{1,0:T(8,128)S(1)} %table.1.table_ref, bf16[1088,128]{1,0:T(8,128)(2,1)S(1)} %bitcast.16, bf16[1088,128]{1,0:T(8,128)(2,1)S(1)} %bitcast.19), custom_call_target="tpu_custom_call" | custom-call | tf_op jit(solution)/shard_map/select/pallas_call | solution.py:246
  32.9 0.0 collective-permute-done.1.mirror_amps_ref
  32.9 0.0 copy-start.1
  32.9 0.0 copy-start.2
  32.9 0.0 copy-start.3
  32.9 31.8 %all_to_all.10 = bf16[128,9,2,128]{3,2,1,0:T(2,128)(2,1)S(1)} all-to-all(bf16[128,9,2,128]{3,2,1,0:T(2,128)(2,1)S(1)} %bitcast.17), channel_id=1, replica_groups=mesh['xa'=2,'xb'=2,'u'=2,'b'=4,'c'=2,'y'=8] {'xb','xa','y','b'}, dimensions={0} | all-to-all | bytes 1179648 | tf_op jit(solution)/shard_map/all_to_all | solution.py:261
  64.8 1.6 %ladder.1 = (bf16[384,384]{1,0:T(8,128)(2,1)S(1)}, bf16[384,768]{1,0:T(8,128)(2,1)S(1)}, bf16[384,768]{1,0:T(8,128)(2,1)S(1)}, bf16[384,768]{1,0:T(8,128)(2,1)S(1)}) custom-call(f32[4,128]{1,0:T(4,128)S(1)} %broadcast_in_dim.2.place_ref, bf16[2,384,384]{2,1,0:T(8,128)(2,1)S(1)} %copy-done, bf16[384,384]{1,0:T(8,128)(2,1)S(1)} %collective-permute-done.1.mirror_amps_ref, ...), custom_call_target="tpu_custom_call" | custom-call | tf_op jit(solution)/shard_map/ladder/pallas_call | solution.py:266
  66.3 2.9 %collective-permute-start.2 = (bf16[384,384]{1,0:T(8,128)(2,1)S(1)}, bf16[384,384]{1,0:T(8,128)(2,1)S(1)}, u32[]{:S(2)}, u32[]{:S(2)}) collective-permute-start(bf16[384,384]{1,0:T(8,128)(2,1)S(1)} %get-tuple-element.13), channel_id=1, source_target_pairs={{256,0},{0,256},{257,1},{1,257},{258,2},{2,258},{259,3},{3,259},{2... | collective-permute-start | bytes 884744 | tf_op jit(solution)/shard_map/ppermute | solution.py:275
  69.2 0.0 copy-done.1
  69.2 0.0 copy-done.2
  69.3 0.0 copy-done.3
  69.3 2.6 %own.1 = (f32[2,384,384]{2,1,0:T(8,128)}, bf16[2,384,384]{2,1,0:T(8,128)(2,1)}, f32[384,384]{1,0:T(8,128)S(1)}) custom-call(s32[4]{0:T(128)S(1)} %get-tuple-element.21.info_ref, s32[3,16]{1,0:T(4,128)S(1)} %bitcast.22, f32[2]{0:T(128)S(1)} %copy-done.3, f32[32,128]{1,0:T(8,128)S(1)} %bitcast.20, bf16[2,384,384]{2,1,0:T(8,128)(2,1)S(1)} %copy-done, ...), custom_call_target="tpu_custom_call" | custom-call | flops 452984832 | bytes 1474560 | tf_op jit(solution)/shard_map/own/pallas_call | solution.py:287
  71.8 4.8 %collective-permute-done.2.received_ref = bf16[384,384]{1,0:T(8,128)(2,1)S(1)} collective-permute-done((bf16[384,384]{1,0:T(8,128)(2,1)S(1)}, bf16[384,384]{1,0:T(8,128)(2,1)S(1)}, u32[]{:S(2)}, u32[]{:S(2)}) %collective-permute-start.2) | collective-permute-done | bytes 294944 | tf_op jit(solution)/shard_map/ppermute | solution.py:275
  76.7 1.1 %other.1 = (f32[2,384,384]{2,1,0:T(8,128)}, bf16[2,384,384]{2,1,0:T(8,128)(2,1)}) custom-call(f32[4,128]{1,0:T(4,128)S(1)} %broadcast_in_dim.2.place_ref, bf16[2,384,384]{2,1,0:T(8,128)(2,1)S(1)} %copy-done, bf16[384,384]{1,0:T(8,128)(2,1)S(1)} %collective-permute-done.2.received_ref, ...), custom_call_target="tpu_custom_call", output_to_operand_aliasing={{0}: (4, {}), {1}: (5, {})} | custom-call | flops 589824 | bytes 1474560 | tf_op jit(solution)/shard_map/other/pallas_call | solution.py:297
  (1 shorter events, 0.0 us)
Async XLA Ops:
  0.6 16.1 %copy-start = (bf16[2,384,384]{2,1,0:T(8,128)(2,1)S(1)}, bf16[2,384,384]{2,1,0:T(8,128)(2,1)}, u32[]{:S(2)}) copy-start(bf16[2,384,384]{2,1,0:T(8,128)(2,1)} %amps_ref.5) | copy-start | bytes 1769476
  2.6 25.1 %all-to-all-start = ((bf16[32,17,2,128]{3,2,1,0:T(2,128)(2,1)}), bf16[32,17,2,128]{3,2,1,0:T(2,128)(2,1)S(1)}, u32[]{:S(2)}, u32[]{:S(2)}) async-start(bf16[32,17,2,128]{3,2,1,0:T(2,128)(2,1)} %bitcast.23), calls=%async_computation | async-start | bytes 557056 | tf_op jit(solution)/shard_map/all_to_all | solution.py:231
  16.8 16.1 %collective-permute-start.1 = (bf16[384,384]{1,0:T(8,128)(2,1)S(1)}, bf16[384,384]{1,0:T(8,128)(2,1)S(1)}, u32[]{:S(2)}, u32[]{:S(2)}) collective-permute-start(bf16[384,384]{1,0:T(8,128)(2,1)S(1)} %dynamic-slice_bitcast_fusion), channel_id=1, source_target_pairs={{256,0},{0,256},{257,1},{1,257},{258,2},{2,258},{259,3},{3,259},{2... | collective-permute-start | bytes 884744 | tf_op jit(solution)/shard_map/ppermute | solution.py:235
  27.7 3.4 %collective-permute-start = (bf16[32,17,2,128]{3,2,1,0:T(2,128)(2,1)S(1)}, bf16[32,17,2,128]{3,2,1,0:T(2,128)(2,1)S(1)}, u32[]{:S(2)}, u32[]{:S(2)}) collective-permute-start(bf16[32,17,2,128]{3,2,1,0:T(2,128)(2,1)S(1)} %all-to-all-done), channel_id=1, source_target_pairs={{8,0},{0,8},{9,1},{1,9},{10,2},{2,10},{11,3},{3,11},{12,4},{4,12},... | collective-permute-start | bytes 835592 | tf_op jit(solution)/shard_map/ppermute | solution.py:232
  32.9 36.3 %copy-start.1 = (f32[4096]{0:T(1024)S(1)}, f32[4096]{0:T(1024)}, u32[]{:S(2)}) copy-start(f32[4096]{0:T(1024)} %param.11) | copy-start | bytes 49156
  32.9 36.3 %copy-start.2 = (s32[16,3]{0,1:T(4,128)S(1)}, s32[16,3]{0,1:T(4,128)}, u32[]{:S(2)}) copy-start(s32[16,3]{0,1:T(4,128)} %param.8) | copy-start | bytes 580
  32.9 36.3 %copy-start.3 = (f32[2]{0:T(128)S(1)}, f32[2]{0:T(128)}, u32[]{:S(2)}) copy-start(f32[2]{0:T(128)} %pair_energy_ref.1) | copy-start | bytes 28
  66.3 10.4 %collective-permute-start.2 = (bf16[384,384]{1,0:T(8,128)(2,1)S(1)}, bf16[384,384]{1,0:T(8,128)(2,1)S(1)}, u32[]{:S(2)}, u32[]{:S(2)}) collective-permute-start(bf16[384,384]{1,0:T(8,128)(2,1)S(1)} %get-tuple-element.13), channel_id=1, source_target_pairs={{256,0},{0,256},{257,1},{1,257},{258,2},{2,258},{259,3},{3,259},{2... | collective-permute-start | bytes 884744 | tf_op jit(solution)/shard_map/ppermute | solution.py:275
